TPU v7x, 32 devices: a whole 2x2x4 slice. The times are simulated.
32 devices in a mesh: fsdp: 8 (over z, y), ctx: 4 (over x, core).
Axes of the slice: x: 2, y: 2, z: 4, core: 2. Of those that a mesh axis runs over, the one named last changes fastest.
Arguments:
- inputs: bfloat16 [8, 1024, 768], P('fsdp', 'ctx'), may hold values from -8 to 8
- cotangent: bfloat16 [8, 1024, 768], P('fsdp', 'ctx'), may hold values from -8 to 8
- block_order: int32 [8], replicated, may hold values from 0 to 7, each once
- norm1_gain: bfloat16 [768], P('fsdp'), may hold values from 0.5 to 1.5
- norm1_shift: bfloat16 [768], P('fsdp'), may hold values from -1.25 to 1.25
- w_qkv: bfloat16 [768, 2304], P('fsdp'), may hold values from -0.21875 to 0.21875
- qv_bias: bfloat16 [2, 768], P(None, 'fsdp'), may hold values from -1.75 to 1.75
- w_out: bfloat16 [768, 768], P('fsdp'), may hold values from -1.75 to 1.75
- out_bias: bfloat16 [768], P('fsdp'), may hold values from -1.25 to 1.25
- norm2_gain: bfloat16 [768], P('fsdp'), may hold values from 0.5 to 1.5
- norm2_shift: bfloat16 [768], P('fsdp'), may hold values from -1.25 to 1.25
- w_fc: bfloat16 [768, 3072], P('fsdp'), may hold values from -0.21875 to 0.21875
- fc_bias: bfloat16 [3072], P('fsdp'), may hold values from -3 to 3
- w_proj: bfloat16 [3072, 768], P('fsdp'), may hold values from -0.109375 to 0.109375
- proj_bias: bfloat16 [768], P('fsdp'), may hold values from -1.25 to 1.25
Outputs:
- output: bfloat16 [8, 1024, 768], P('fsdp', 'ctx')
- input_grad: bfloat16 [8, 1024, 768], P('fsdp', 'ctx')
- norm1_gain_grad: float32 [768], P('fsdp')
- norm1_shift_grad: float32 [768], P('fsdp')
- w_qkv_grad: float32 [768, 2304], P('fsdp')
- qv_bias_grad: float32 [2, 768], P(None, 'fsdp')
- w_out_grad: float32 [768, 768], P('fsdp')
- out_bias_grad: float32 [768], P('fsdp')
- norm2_gain_grad: float32 [768], P('fsdp')
- norm2_shift_grad: float32 [768], P('fsdp')
- w_fc_grad: float32 [768, 3072], P('fsdp')
- fc_bias_grad: float32 [3072], P('fsdp')
- w_proj_grad: float32 [3072, 768], P('fsdp')
- proj_bias_grad: float32 [768], P('fsdp')
Inputs may be any that keep to these rules, and one draw needn't show every extreme that they name: block_order names each of the 128-token position blocks of a sequence once.
All inputs are finite; a program needn't handle non-finite values.
Results may differ from a plain program's by a relative error of at most 0.02.
Values may be sent and summed in bfloat16 or wider, within the bound.
A program may use at most 128 MiB of HBM per device.

v0:
```python
from functools import partial

import jax
import jax.numpy as jnp
from jax import lax
from jax.sharding import PartitionSpec as P

HEADS = 12


EPS = 1e-05
LOWEST = -1e30


def layer_norm(values, gain, shift):
    centre = jnp.mean(values, axis=-1, keepdims=True)
    centred = values - centre
    spread = jnp.mean(centred * centred, axis=-1, keepdims=True)
    return centred * lax.rsqrt(spread + EPS) * gain + shift


def block_places(block_order, first_row, row_count, block_rows):
    row_index = first_row + jnp.arange(row_count, dtype=jnp.int32)
    which_block = row_index // block_rows
    table = jnp.arange(block_order.shape[0], dtype=jnp.int32)
    picked = jnp.sum(
        jnp.where(which_block[:, None] == table[None, :], block_order[None, :], 0), axis=1
    )
    return picked * block_rows + row_index % block_rows


def keep_same(current):
    return current


def shards(
    inputs,
    cotangent,
    block_order,
    norm1_gain,
    norm1_shift,
    w_qkv,
    qv_bias,
    w_out,
    out_bias,
    norm2_gain,
    norm2_shift,
    w_fc,
    fc_bias,
    w_proj,
    proj_bias,
):
    local_rows = inputs.shape[1]
    model_width = inputs.shape[2]
    block_rows = local_rows // 2
    head_dim = model_width // HEADS
    score_scale = head_dim ** (-0.5)
    row_offset = lax.axis_index("ctx") * local_rows
    query_places = block_places(block_order, row_offset, local_rows, block_rows)
    gathered = (
        lax.all_gather(norm1_gain, "fsdp", axis=0, tiled=True),
        lax.all_gather(norm1_shift, "fsdp", axis=0, tiled=True),
        lax.all_gather(w_qkv, "fsdp", axis=0, tiled=True),
        lax.all_gather(qv_bias, "fsdp", axis=1, tiled=True),
        lax.all_gather(w_out, "fsdp", axis=0, tiled=True),
        lax.all_gather(out_bias, "fsdp", axis=0, tiled=True),
        lax.all_gather(norm2_gain, "fsdp", axis=0, tiled=True),
        lax.all_gather(norm2_shift, "fsdp", axis=0, tiled=True),
        lax.all_gather(w_fc, "fsdp", axis=0, tiled=True),
        lax.all_gather(fc_bias, "fsdp", axis=0, tiled=True),
        lax.all_gather(w_proj, "fsdp", axis=0, tiled=True),
        lax.all_gather(proj_bias, "fsdp", axis=0, tiled=True),
    )
    (
        gain_one,
        shift_one,
        qkv_weight,
        bias_pair,
        out_weight,
        out_shift,
        gain_two,
        shift_two,
        fc_weight,
        fc_shift,
        proj_weight,
        proj_shift,
    ) = gathered
    tokens = inputs[0].astype(jnp.float32)
    normed_one, norm_one_back = jax.vjp(
        layer_norm, tokens, gain_one.astype(jnp.float32), shift_one.astype(jnp.float32)
    )
    normed_one_low = normed_one.astype(jnp.bfloat16)
    qkv_shift = jnp.concatenate([bias_pair[0], jnp.zeros_like(bias_pair[0]), bias_pair[1]]).astype(
        jnp.float32
    )
    qkv_low = (
        jnp.dot(normed_one_low, qkv_weight, preferred_element_type=jnp.float32) + qkv_shift
    ).astype(jnp.bfloat16)
    queries = qkv_low[:, :model_width].reshape(local_rows, HEADS, head_dim)
    key_value = qkv_low[:, model_width:]
    start_state = (
        jnp.full((HEADS, local_rows), LOWEST, jnp.float32),
        jnp.zeros((HEADS, local_rows), jnp.float32),
        jnp.zeros((local_rows, HEADS, head_dim), jnp.float32),
    )
    arrived = lax.all_gather(key_value, "ctx", axis=0, tiled=True)
    arrived_rows = arrived.shape[0]
    key_places = block_places(block_order, jnp.int32(0), arrived_rows, block_rows)
    arrived_keys = arrived[:, :model_width].reshape(arrived_rows, HEADS, head_dim)
    arrived_values = arrived[:, model_width:].reshape(arrived_rows, HEADS, head_dim)
    lowest_key = jnp.min(key_places)
    updated = []
    for local_block in range(2):
        row_begin = local_block * block_rows
        row_end = row_begin + block_rows
        block_queries = queries[row_begin:row_end]
        own_places = query_places[row_begin:row_end]

        def attend(current):
            old_high, old_total, old_sum = current
            scores = (
                jnp.einsum(
                    "thd,shd->hts", block_queries, arrived_keys, preferred_element_type=jnp.float32
                )
                * score_scale
            )
            visible = key_places[None, None, :] <= own_places[None, :, None]
            scores = jnp.where(visible, scores, -jnp.inf)
            new_high = jnp.maximum(old_high, jnp.max(scores, axis=2))
            factor = jnp.exp(old_high - new_high)
            shares = jnp.exp(scores - new_high[:, :, None])
            new_total = jnp.sum(shares, axis=2)
            addition = jnp.einsum(
                "hts,shd->thd",
                shares.astype(jnp.bfloat16),
                arrived_values,
                preferred_element_type=jnp.float32,
            )
            return (new_high, new_total, old_sum * factor.T[:, :, None] + addition)

        current = (
            start_state[0][:, row_begin:row_end],
            start_state[1][:, row_begin:row_end],
            start_state[2][row_begin:row_end],
        )
        needed = lowest_key <= jnp.max(own_places)
        updated.append(lax.cond(needed, attend, keep_same, current))
    highest = jnp.concatenate([updated[0][0], updated[1][0]], axis=1)
    denominator = jnp.concatenate([updated[0][1], updated[1][1]], axis=1)
    summed = jnp.concatenate([updated[0][2], updated[1][2]], axis=0)
    attended = (summed / denominator.T[:, :, None]).reshape(local_rows, model_width)
    attended_low = attended.astype(jnp.bfloat16)
    log_total = highest + jnp.log(denominator)
    middle = (
        tokens
        + jnp.dot(attended_low, out_weight, preferred_element_type=jnp.float32)
        + out_shift.astype(jnp.float32)
    )
    normed_two, norm_two_back = jax.vjp(
        layer_norm, middle, gain_two.astype(jnp.float32), shift_two.astype(jnp.float32)
    )
    normed_two_low = normed_two.astype(jnp.bfloat16)
    hidden = jnp.dot(
        normed_two_low, fc_weight, preferred_element_type=jnp.float32
    ) + fc_shift.astype(jnp.float32)
    activated, gelu_back = jax.vjp(partial(jax.nn.gelu, approximate=True), hidden)
    activated_low = activated.astype(jnp.bfloat16)
    output = (
        middle
        + jnp.dot(activated_low, proj_weight, preferred_element_type=jnp.float32)
        + proj_shift.astype(jnp.float32)
    )
    again = (
        lax.all_gather(norm1_gain, "fsdp", axis=0, tiled=True),
        lax.all_gather(norm1_shift, "fsdp", axis=0, tiled=True),
        lax.all_gather(w_qkv, "fsdp", axis=0, tiled=True),
        lax.all_gather(qv_bias, "fsdp", axis=1, tiled=True),
        lax.all_gather(w_out, "fsdp", axis=0, tiled=True),
        lax.all_gather(out_bias, "fsdp", axis=0, tiled=True),
        lax.all_gather(norm2_gain, "fsdp", axis=0, tiled=True),
        lax.all_gather(norm2_shift, "fsdp", axis=0, tiled=True),
        lax.all_gather(w_fc, "fsdp", axis=0, tiled=True),
        lax.all_gather(fc_bias, "fsdp", axis=0, tiled=True),
        lax.all_gather(w_proj, "fsdp", axis=0, tiled=True),
        lax.all_gather(proj_bias, "fsdp", axis=0, tiled=True),
    )
    qkv_back = again[2]
    out_back = again[4]
    fc_back = again[8]
    proj_back = again[10]
    grad_output = cotangent[0]
    grad_proj_weight = jnp.dot(activated_low.T, grad_output, preferred_element_type=jnp.float32)
    grad_proj_shift = jnp.sum(grad_output, axis=0, dtype=jnp.float32)
    grad_activated = jnp.dot(grad_output, proj_back.T, preferred_element_type=jnp.float32)
    (grad_hidden,) = gelu_back(grad_activated)
    grad_hidden_low = grad_hidden.astype(jnp.bfloat16)
    grad_fc_weight = jnp.dot(normed_two_low.T, grad_hidden_low, preferred_element_type=jnp.float32)
    grad_fc_shift = jnp.sum(grad_hidden_low, axis=0, dtype=jnp.float32)
    grad_normed_two = jnp.dot(grad_hidden_low, fc_back.T, preferred_element_type=jnp.float32)
    grad_middle_norm, grad_gain_two, grad_shift_two = norm_two_back(grad_normed_two)
    grad_middle = grad_output.astype(jnp.float32) + grad_middle_norm
    grad_branch_low = grad_middle.astype(jnp.bfloat16)
    grad_out_weight = jnp.dot(attended_low.T, grad_branch_low, preferred_element_type=jnp.float32)
    grad_out_shift = jnp.sum(grad_branch_low, axis=0, dtype=jnp.float32)
    grad_attended_low = jnp.dot(
        grad_branch_low, out_back.T, preferred_element_type=jnp.float32
    ).astype(jnp.bfloat16)
    grad_attended_heads = grad_attended_low.reshape(local_rows, HEADS, head_dim)
    delta = jnp.sum(
        grad_attended_heads.astype(jnp.float32) * attended.reshape(local_rows, HEADS, head_dim),
        axis=2,
    ).T
    arrived = lax.all_gather(key_value, "ctx", axis=0, tiled=True)
    grad_queries = jnp.zeros((local_rows, HEADS, head_dim), jnp.float32)
    arrived_rows = arrived.shape[0]
    backward_key_places = block_places(block_order, jnp.int32(0), arrived_rows, block_rows)
    backward_arrived_keys = arrived[:, :model_width].reshape(arrived_rows, HEADS, head_dim)
    backward_arrived_values = arrived[:, model_width:].reshape(arrived_rows, HEADS, head_dim)
    lowest_key = jnp.min(backward_key_places)
    key_total = jnp.zeros((arrived_rows, HEADS, head_dim), jnp.float32)
    value_total = jnp.zeros((arrived_rows, HEADS, head_dim), jnp.float32)
    query_parts = []
    for local_block in range(2):
        row_begin = local_block * block_rows
        row_end = row_begin + block_rows
        backward_block_queries = queries[row_begin:row_end]
        backward_own_places = query_places[row_begin:row_end]
        own_log = log_total[:, row_begin:row_end]
        own_delta = delta[:, row_begin:row_end]
        own_grad = grad_attended_heads[row_begin:row_end]

        def differentiate(current):
            block_grad, key_sum, value_sum = current
            scores = (
                jnp.einsum(
                    "thd,shd->hts",
                    backward_block_queries,
                    backward_arrived_keys,
                    preferred_element_type=jnp.float32,
                )
                * score_scale
            )
            visible = backward_key_places[None, None, :] <= backward_own_places[None, :, None]
            shares = jnp.where(visible, jnp.exp(scores - own_log[:, :, None]), 0.0)
            value_sum = value_sum + jnp.einsum(
                "hts,thd->shd",
                shares.astype(jnp.bfloat16),
                own_grad,
                preferred_element_type=jnp.float32,
            )
            grad_shares = jnp.einsum(
                "thd,shd->hts",
                own_grad,
                backward_arrived_values,
                preferred_element_type=jnp.float32,
            )
            grad_scores = (shares * (grad_shares - own_delta[:, :, None])).astype(jnp.bfloat16)
            block_grad = (
                jnp.einsum(
                    "hts,shd->thd",
                    grad_scores,
                    backward_arrived_keys,
                    preferred_element_type=jnp.float32,
                )
                * score_scale
            )
            key_sum = (
                key_sum
                + jnp.einsum(
                    "hts,thd->shd",
                    grad_scores,
                    backward_block_queries,
                    preferred_element_type=jnp.float32,
                )
                * score_scale
            )
            return (block_grad, key_sum, value_sum)

        current = (grad_queries[row_begin:row_end], key_total, value_total)
        needed = lowest_key <= jnp.max(backward_own_places)
        block_grad, key_total, value_total = lax.cond(needed, differentiate, keep_same, current)
        query_parts.append(block_grad)
    addition = jnp.concatenate(
        [
            key_total.reshape(arrived_rows, model_width),
            value_total.reshape(arrived_rows, model_width),
        ],
        axis=1,
    )
    grad_keys_values = addition
    grad_queries, grad_keys_values = (jnp.concatenate(query_parts, axis=0), grad_keys_values)
    grad_kv_local = lax.psum_scatter(
        grad_keys_values.astype(jnp.bfloat16), "ctx", scatter_dimension=0, tiled=True
    ).astype(jnp.float32)
    grad_qkv_low = jnp.concatenate(
        [grad_queries.reshape(local_rows, model_width), grad_kv_local], axis=1
    ).astype(jnp.bfloat16)
    grad_qkv_weight = jnp.dot(normed_one_low.T, grad_qkv_low, preferred_element_type=jnp.float32)
    column_sums = jnp.sum(grad_qkv_low, axis=0, dtype=jnp.float32)
    grad_bias_pair = jnp.stack([column_sums[:model_width], column_sums[2 * model_width :]])
    grad_normed_one = jnp.dot(grad_qkv_low, qkv_back.T, preferred_element_type=jnp.float32)
    grad_tokens_norm, grad_gain_one, grad_shift_one = norm_one_back(grad_normed_one)
    grad_tokens = grad_middle + grad_tokens_norm
    shard_grads = (
        lax.psum_scatter(
            grad_gain_one.astype(jnp.bfloat16), "fsdp", scatter_dimension=0, tiled=True
        ).astype(jnp.float32),
        lax.psum_scatter(
            grad_shift_one.astype(jnp.bfloat16), "fsdp", scatter_dimension=0, tiled=True
        ).astype(jnp.float32),
        lax.psum_scatter(
            grad_qkv_weight.astype(jnp.bfloat16), "fsdp", scatter_dimension=0, tiled=True
        ).astype(jnp.float32),
        lax.psum_scatter(
            grad_bias_pair.astype(jnp.bfloat16), "fsdp", scatter_dimension=1, tiled=True
        ).astype(jnp.float32),
        lax.psum_scatter(
            grad_out_weight.astype(jnp.bfloat16), "fsdp", scatter_dimension=0, tiled=True
        ).astype(jnp.float32),
        lax.psum_scatter(
            grad_out_shift.astype(jnp.bfloat16), "fsdp", scatter_dimension=0, tiled=True
        ).astype(jnp.float32),
        lax.psum_scatter(
            grad_gain_two.astype(jnp.bfloat16), "fsdp", scatter_dimension=0, tiled=True
        ).astype(jnp.float32),
        lax.psum_scatter(
            grad_shift_two.astype(jnp.bfloat16), "fsdp", scatter_dimension=0, tiled=True
        ).astype(jnp.float32),
        lax.psum_scatter(
            grad_fc_weight.astype(jnp.bfloat16), "fsdp", scatter_dimension=0, tiled=True
        ).astype(jnp.float32),
        lax.psum_scatter(
            grad_fc_shift.astype(jnp.bfloat16), "fsdp", scatter_dimension=0, tiled=True
        ).astype(jnp.float32),
        lax.psum_scatter(
            grad_proj_weight.astype(jnp.bfloat16), "fsdp", scatter_dimension=0, tiled=True
        ).astype(jnp.float32),
        lax.psum_scatter(
            grad_proj_shift.astype(jnp.bfloat16), "fsdp", scatter_dimension=0, tiled=True
        ).astype(jnp.float32),
    )
    summed_grads = (
        lax.psum(shard_grads[0].astype(jnp.bfloat16), "ctx").astype(jnp.float32),
        lax.psum(shard_grads[1].astype(jnp.bfloat16), "ctx").astype(jnp.float32),
        lax.psum(shard_grads[2].astype(jnp.bfloat16), "ctx").astype(jnp.float32),
        lax.psum(shard_grads[3].astype(jnp.bfloat16), "ctx").astype(jnp.float32),
        lax.psum(shard_grads[4].astype(jnp.bfloat16), "ctx").astype(jnp.float32),
        lax.psum(shard_grads[5].astype(jnp.bfloat16), "ctx").astype(jnp.float32),
        lax.psum(shard_grads[6].astype(jnp.bfloat16), "ctx").astype(jnp.float32),
        lax.psum(shard_grads[7].astype(jnp.bfloat16), "ctx").astype(jnp.float32),
        lax.psum(shard_grads[8].astype(jnp.bfloat16), "ctx").astype(jnp.float32),
        lax.psum(shard_grads[9].astype(jnp.bfloat16), "ctx").astype(jnp.float32),
        lax.psum(shard_grads[10].astype(jnp.bfloat16), "ctx").astype(jnp.float32),
        lax.psum(shard_grads[11].astype(jnp.bfloat16), "ctx").astype(jnp.float32),
    )
    return (
        output[None].astype(jnp.bfloat16),
        grad_tokens[None].astype(jnp.bfloat16),
        summed_grads[0],
        summed_grads[1],
        summed_grads[2],
        summed_grads[3],
        summed_grads[4],
        summed_grads[5],
        summed_grads[6],
        summed_grads[7],
        summed_grads[8],
        summed_grads[9],
        summed_grads[10],
        summed_grads[11],
    )


def solution(mesh):
    in_specs = (
        P("fsdp", "ctx", None),
        P("fsdp", "ctx", None),
        P(),
        P("fsdp"),
        P("fsdp"),
        P("fsdp", None),
        P(None, "fsdp"),
        P("fsdp", None),
        P("fsdp"),
        P("fsdp"),
        P("fsdp"),
        P("fsdp", None),
        P("fsdp"),
        P("fsdp", None),
        P("fsdp"),
    )
    out_specs = (
        P("fsdp", "ctx", None),
        P("fsdp", "ctx", None),
        P("fsdp"),
        P("fsdp"),
        P("fsdp", None),
        P(None, "fsdp"),
        P("fsdp", None),
        P("fsdp"),
        P("fsdp"),
        P("fsdp"),
        P("fsdp", None),
        P("fsdp"),
        P("fsdp", None),
        P("fsdp"),
    )
    return jax.shard_map(shards, mesh=mesh, in_specs=in_specs, out_specs=out_specs, check_vma=False)
```

profile of v0, /device:TPU:0, one launch (start us, length us, event | category | flops | bytes accessed | tf_op | source)
XLA Modules:
  0.0 892.4 jit_solution(1225135298237572399)
XLA Ops:
  14.1 39.6 %all-reduce.14 = (bf16[768]{0:T(1024)(128)(2,1)S(1)}, bf16[768]{0:T(1024)(128)(2,1)S(1)}, bf16[768]{0:T(1024)(128)(2,1)S(1)}, bf16[768]{0:T(1024)(128)(2,1)S(1)}, bf16[768]{0:T(1024)(128)(2,1)S(1)}) all-reduce(bf16[768]{0:T(1024)(128)(2,1)S(1)} %dynamic-update-slice.1, ...), channel_id=1, replica_groups=mesh['fsdp'=8,'ctx'=4] {'fsdp'}, use_global_device_ids=true, to_apply=%add.1 | all-reduce | flops 3840 | bytes 15360
  53.7 16.6 %all-gather = bf16[8,96,2]{1,2,0:T(2,128)(2,1)S(1)} all-gather(bf16[1,96,2]{1,2,0:T(2,128)(2,1)} %bitcast.171), channel_id=1, replica_groups=mesh['fsdp'=8,'ctx'=4] {'fsdp'}, dimensions={0}, use_global_device_ids=true | all-gather | bytes 3456 | tf_op jit(solution)/shard_map/all_gather | solution.py:64
  72.9 5.8 all-gather.8.cloned.1.call-done
  78.7 3.3 fusion.55
  90.9 25.9 %all-gather.1 = bf16[8,1,384]{2,1,0:T(2,128)(2,1)S(1)} all-gather(bf16[1,1,384]{2,1,0:T(2,128)(2,1)S(1)} %reshape.351), channel_id=1, replica_groups=mesh['fsdp'=8,'ctx'=4] {'fsdp'}, dimensions={0}, use_global_device_ids=true | all-gather | bytes 6912 | tf_op jit(solution)/shard_map/all_gather | solution.py:70
  118.4 2.1 fusion.114
  124.0 8.6 conditional.4
  126.0 3.3 fusion.9
  129.3 2.3 fusion.2
  132.6 8.8 conditional.5
  134.8 3.3 fusion.23
  138.1 2.3 fusion.16
  142.0 11.5 %all-gather.12.cloned.1.call-done = bf16[768,768]{1,0:T(8,128)(2,1)} async-done(((bf16[96,768]{1,0:T(8,128)(2,1)}), bf16[768,768]{1,0:T(8,128)(2,1)}) %all-gather.12.cloned.1.call-update) | async-done | bytes 1179664 | tf_op jit(solution)/shard_map/all_gather | solution.py:65
  155.6 78.6 %all-gather.14.cloned.1.call-done = bf16[768,3072]{1,0:T(8,128)(2,1)} async-done(((bf16[96,3072]{1,0:T(8,128)(2,1)}), bf16[768,3072]{1,0:T(8,128)(2,1)}) %all-gather.14.cloned.1.call-update) | async-done | bytes 4718608 | tf_op jit(solution)/shard_map/all_gather | solution.py:69
  234.2 5.5 convolution_add_fusion.1
  239.8 74.5 %all-gather.16.cloned.1.call-done = bf16[3072,768]{1,0:T(8,128)(2,1)} async-done(((bf16[384,768]{1,0:T(8,128)(2,1)}), bf16[3072,768]{1,0:T(8,128)(2,1)}) %all-gather.16.cloned.1.call-update) | async-done | bytes 4718608 | tf_op jit(solution)/shard_map/all_gather | solution.py:71
  314.3 7.5 fusion.119
  321.8 2.2 multiply_reduce_fusion
  327.9 2.0 copy.65
  332.8 18.0 %conditional.6 = (f32[1024,12,64]{0,2,1:T(8,128)}, f32[1024,12,64]{0,2,1:T(8,128)}, bf16[128,12,64]{0,2,1:T(8,128)(2,1)}) conditional(s32[]{:T(128)} %convert_element_type.204, () %tuple.44, (s32[1024]{0:T(1024)}, s32[128]{0:T(128)}, bf16[128,12,64]{0,2,1:T(8,128)(2,1)}, bf16[1024,12,64]{0,2,1:T(8,128)(2,1)S(1)}, f32[12,256]{1,0:T(8,128)S(1)}, ...), branch_computations={%region_20.21_spmd, %region_21.22_spmd} | conditional | flops 1023475712 | bytes 49576612 | solution.py:281
  338.6 2.1 fusion.120
  340.7 2.7 multiply_convert_fusion
  343.4 3.2 fusion.35
  346.6 2.0 fusion.39
  348.6 2.2 multiply_bitcast_fusion.2
  350.8 22.6 %conditional.7 = (f32[1024,12,64]{0,2,1:T(8,128)}, f32[1024,12,64]{0,2,1:T(8,128)}, bf16[128,12,64]{0,2,1:T(8,128)(2,1)}) conditional(s32[]{:T(128)} %convert_element_type.210, (f32[1024,12,64]{0,2,1:T(8,128)}, f32[1024,12,64]{0,2,1:T(8,128)}) %tuple.46, (s32[1024]{0:T(1024)}, s32[128]{0:T(128)}, bf16[128,12,64]{0,2,1:T(8,128)(2,1)}, ...), branch_computations={%region_22.23_spmd, %region_23.24_spmd} | conditional | flops 1025048576 | bytes 55868068 | solution.py:281
  359.8 4.7 bitcast_add_fusion
  364.5 2.6 multiply_convert_fusion.1
  367.1 2.0 fusion.52
  369.1 4.3 bitcast_add_fusion.1
  373.4 2.1 convert.31
  375.5 2.1 convert.32
  382.5 5.5 convolution_convert_fusion.1
  389.0 6.4 convolution_convert_fusion
  396.7 19.2 %reduce-scatter.9.cloned.1.call-done = bf16[256,1536]{0,1:T(8,128)(2,1)} async-done(((bf16[1024,1536]{0,1:T(8,128)(2,1)}), bf16[256,1536]{0,1:T(8,128)(2,1)}) %reduce-scatter.9.cloned.1.call-update) | async-done | bytes 786448 | tf_op jit(solution)/shard_map/reduce_scatter | solution.py:292
  415.9 4.2 convolution_convert_fusion.2
  424.5 4.1 fusion.108
  429.1 38.0 %all-reduce.13 = (bf16[768]{0:T(1024)(128)(2,1)S(1)}, bf16[768]{0:T(1024)(128)(2,1)S(1)}, bf16[768]{0:T(1024)(128)(2,1)S(1)}, bf16[768]{0:T(1024)(128)(2,1)S(1)}...) all-reduce(bf16[768]{0:T(1024)(128)(2,1)} %copy-done.41, ...), channel_id=1, replica_groups=mesh['fsdp'=8,'ctx'=4] {'fsdp'}, use_global_device_ids=true, to_apply=%add.5 | all-reduce | flops 8448 | bytes 33792
  467.6 17.0 %reduce-scatter.13.cloned.1.call-done = bf16[96,768]{1,0:T(8,128)(2,1)} async-done(((bf16[768,768]{1,0:T(8,128)(2,1)}), bf16[96,768]{1,0:T(8,128)(2,1)}) %reduce-scatter.13.cloned.1.call-update) | async-done | bytes 147472 | tf_op jit(solution)/shard_map/reduce_scatter | solution.py:317
  484.6 98.5 %reduce-scatter.15.cloned.1.call-done = bf16[96,3072]{1,0:T(8,128)(2,1)} async-done(((bf16[768,3072]{1,0:T(8,128)(2,1)}), bf16[96,3072]{1,0:T(8,128)(2,1)}) %reduce-scatter.15.cloned.1.call-update) | async-done | bytes 589840 | tf_op jit(solution)/shard_map/reduce_scatter | solution.py:329
  583.1 99.3 %reduce-scatter.17.cloned.1.call-done = bf16[384,768]{1,0:T(8,128)(2,1)} async-done(((bf16[3072,768]{1,0:T(8,128)(2,1)}), bf16[384,768]{1,0:T(8,128)(2,1)}) %reduce-scatter.17.cloned.1.call-update) | async-done | bytes 589840 | tf_op jit(solution)/shard_map/reduce_scatter | solution.py:335
  682.4 82.7 %reduce-scatter.11.cloned.1.call-done = bf16[96,2304]{1,0:T(8,128)(2,1)} async-done(((bf16[768,2304]{1,0:T(8,128)(2,1)}), bf16[96,2304]{1,0:T(8,128)(2,1)}) %reduce-scatter.11.cloned.1.call-update) | async-done | bytes 442384 | tf_op jit(solution)/shard_map/reduce_scatter | solution.py:311
  766.2 6.0 fusion.66
  772.2 57.6 %reduce-scatter.19.cloned.1.call-done = bf16[96,2]{1,0:T(8,128)(2,1)} async-done(((bf16[768,2]{1,0:T(8,128)(2,1)}), bf16[96,2]{1,0:T(8,128)(2,1)}) %reduce-scatter.19.cloned.1.call-update) | async-done | bytes 400
  830.6 5.7 all-reduce.15
  840.6 37.5 %all-reduce.19.cloned.1.call-done = (bf16[96,2304]{1,0:T(8,128)(2,1)}, bf16[96,768]{1,0:T(8,128)(2,1)}, bf16[96,3072]{1,0:T(8,128)(2,1)}, bf16[384,768]{1,0:T(8,128)(2,1)}) async-done(((bf16[96,2304]{1,0:T(8,128)(2,1)}, bf16[96,768]{1,0:T(8,128)(2,1)}, bf16[96,3072]{1,0:T(8,128)(2,1)}, bf16[384,768]{1,0:T(8,128)(2,1)}), (bf16[96,2304]{1,0:T(8,128)(2,1)}, bf16[96,768]{1,0:T(8,128)(2,1)}, ...) | async-done | bytes 1769488 | tf_op jit(solution)/shard_map/psum | solution.py:345
  879.9 2.0 convert_element_type.234
  881.8 2.2 convert_element_type.245
  (231 shorter events, 69.8 us)
Async XLA Ops:
  7.2 71.5 %all-gather.8.cloned.1.call-start = ((), (), s32[]{:S(2)}) async-start(), calls=%async_computation.6 | async-start | bytes 3981312 | tf_op jit(solution)/shard_map/all_gather | solution.py:63
  7.9 110.5 %all-gather.10.cloned.1.call-start = ((), (), s32[]{:S(2)}) async-start(), calls=%async_computation.7 | async-start | bytes 3932160 | tf_op jit(solution)/shard_map/all_gather | solution.py:106
  71.6 10.4 %copy-start.27 = (f32[256]{0:T(256)}, f32[256]{0:T(256)S(1)}, u32[]{:S(2)}) copy-start(f32[256]{0:T(256)S(1)} %broadcast_multiply_fusion.1) | copy-start | bytes 3076
  72.9 9.1 %copy-start.39 = (f32[256]{0:T(256)}, f32[256]{0:T(256)S(1)}, u32[]{:S(2)}) copy-start(f32[256]{0:T(256)S(1)} %fusion.77) | copy-start | bytes 3076
  72.9 9.1 %copy-start.31 = (f32[256]{0:T(256)}, f32[256]{0:T(256)S(1)}, u32[]{:S(2)}) copy-start(f32[256]{0:T(256)S(1)} %fusion.101) | copy-start | bytes 3076
  82.0 2.9 copy-start.47
  82.0 3.6 copy-start.46
  83.0 70.5 %all-gather.12.cloned.1.call-start = ((), (), s32[]{:S(2)}) async-start(), calls=%async_computation.8 | async-start | bytes 1327104 | tf_op jit(solution)/shard_map/all_gather | solution.py:65
  83.7 150.5 %all-gather.14.cloned.1.call-start = ((), (), s32[]{:S(2)}) async-start(), calls=%async_computation.9 | async-start | bytes 5308416 | tf_op jit(solution)/shard_map/all_gather | solution.py:69
  84.3 230.0 %all-gather.16.cloned.1.call-start = ((), (), s32[]{:S(2)}) async-start(), calls=%async_computation.10 | async-start | bytes 5308416 | tf_op jit(solution)/shard_map/all_gather | solution.py:71
  84.9 331.0 %reduce-scatter.9.cloned.1.call-start = ((), (), s32[]{:S(2)}) async-start(), calls=%async_computation.11 | async-start | bytes 3932160 | tf_op jit(solution)/shard_map/reduce_scatter | solution.py:292
  117.6 5.5 copy-start.9
  120.6 2.4 copy-start.23
  120.6 2.4 copy-start.45
  124.1 1.8 copy-start.14
  132.6 20.9 %copy-start = (bf16[1,256,768]{2,1,0:T(8,128)(2,1)S(1)}, bf16[1,256,768]{2,1,0:T(8,128)(2,1)}, u32[]{:S(2)}) copy-start(bf16[1,256,768]{2,1,0:T(8,128)(2,1)} %param.23) | copy-start | bytes 1179652
  142.0 92.2 %copy-start.5 = (bf16[256,768]{0,1:T(8,128)(2,1)}, bf16[256,768]{0,1:T(8,128)(2,1)S(1)}, u32[]{:S(2)}) copy-start(bf16[256,768]{0,1:T(8,128)(2,1)S(1)} %fusion.79) | copy-start | bytes 1179652
  155.4 166.4 %copy-start.33 = (f32[256]{0:T(256)}, f32[256]{0:T(256)S(1)}, u32[]{:S(2)}) copy-start(f32[256]{0:T(256)S(1)} %broadcast_multiply_fusion) | copy-start | bytes 3076
  155.6 166.2 %copy-start.35 = (f32[256]{0:T(256)}, f32[256]{0:T(256)S(1)}, u32[]{:S(2)}) copy-start(f32[256]{0:T(256)S(1)} %fusion.102) | copy-start | bytes 3076
  234.2 80.1 %copy-start.2 = (bf16[1,256,768]{2,1,0:T(8,128)(2,1)S(1)}, bf16[1,256,768]{2,1,0:T(8,128)(2,1)}, u32[]{:S(2)}) copy-start(bf16[1,256,768]{2,1,0:T(8,128)(2,1)} %param.24) | copy-start | bytes 1179652
  314.3 7.5 copy-start.48
  321.8 2.2 copy-start.18
  321.8 3.3 copy-start.3
  324.0 2.7 copy-start.1
  338.5 2.1 copy-start.16
  338.5 2.1 copy-start.21
  338.5 2.1 copy-start.30
  338.6 2.1 copy-start.43
  346.6 2.0 copy-start.10
  357.7 2.0 copy-start.20
  357.7 2.0 copy-start.29
  359.8 4.7 copy-start.17
  359.8 4.7 copy-start.42
  367.1 2.0 copy-start.13
  379.6 2.9 copy-start.34
  379.6 2.9 copy-start.36
  379.6 105.0 %reduce-scatter.13.cloned.1.call-start = ((), (), s32[]{:S(2)}) async-start(), calls=%async_computation.13 | async-start | bytes 1327104 | tf_op jit(solution)/shard_map/reduce_scatter | solution.py:317
  382.2 200.9 %reduce-scatter.15.cloned.1.call-start = ((), (), s32[]{:S(2)}) async-start(), calls=%async_computation.14 | async-start | bytes 5308416 | tf_op jit(solution)/shard_map/reduce_scatter | solution.py:329
  388.1 294.3 %reduce-scatter.17.cloned.1.call-start = ((), (), s32[]{:S(2)}) async-start(), calls=%async_computation.15 | async-start | bytes 5308416 | tf_op jit(solution)/shard_map/reduce_scatter | solution.py:335
  395.4 20.5 %copy-start.28 = (f32[256]{0:T(256)S(1)}, f32[256]{0:T(256)}, u32[]{:S(2)}) copy-start(f32[256]{0:T(256)} %copy-done.27) | copy-start | bytes 3076
  395.4 20.5 %copy-start.32 = (f32[256]{0:T(256)S(1)}, f32[256]{0:T(256)}, u32[]{:S(2)}) copy-start(f32[256]{0:T(256)} %copy-done.31) | copy-start | bytes 3076
  395.5 369.6 %reduce-scatter.11.cloned.1.call-start = ((), (), s32[]{:S(2)}) async-start(), calls=%async_computation.12 | async-start | bytes 3981312 | tf_op jit(solution)/shard_map/reduce_scatter | solution.py:311
  420.1 2.9 copy-start.11
  420.1 409.7 %reduce-scatter.19.cloned.1.call-start = ((), (), s32[]{:S(2)}) async-start(), calls=%async_computation.16 | async-start | bytes 221184
  424.5 4.1 copy-start.40
  428.5 336.5 %copy-start.38 = (f32[256]{0:T(256)S(1)}, f32[256]{0:T(256)}, u32[]{:S(2)}) copy-start(f32[256]{0:T(256)} %copy-done.37) | copy-start | bytes 3076
  429.0 449.1 %all-reduce.19.cloned.1.call-start = ((), (), s32[]{:S(2)}) async-start(), calls=%async_computation.17 | async-start | bytes 3538944 | tf_op jit(solution)/shard_map/psum | solution.py:345
  878.1 5.9 copy-start.19
  (13 other events, 12.5 us)
Sparse Core Ops, SparseCore 0:
  10.2 68.4 all-gather.7
  83.1 27.0 all-gather.9
  112.4 41.0 all-gather.11
  155.5 78.6 all-gather.13
  236.2 78.0 all-gather.15
  379.8 36.0 reduce-scatter.8
  420.2 64.3 reduce-scatter.12
  488.7 94.3 reduce-scatter.14
  587.2 95.1 reduce-scatter.16
  686.3 78.7 reduce-scatter.10
  769.2 60.5 reduce-scatter.18
  832.5 45.6 all-reduce.18
where the time goes:
time: 900 us; the launch traced here: 892 us
  waiting for transfers between devices  585 us (65%)
  blocking collectives  126 us (14%)
  matrix products  86 us (10%)
  other arithmetic  41 us (5%)
  local copies, waits for them, and re-layouts  33.7 us (4%)
  between operations  19.8 us (2%)
    reduce_scatter x1, waiting for transfers between devices, shards(): lax.psum_scatter(grad_proj_weight.astype(jnp.bfloat16), 'fsdp', scatter_d...  99.3 us
    reduce_scatter x1, waiting for transfers between devices, shards(): lax.psum_scatter(grad_fc_weight.astype(jnp.bfloat16), 'fsdp', scatter_dim...  98.5 us
    reduce_scatter x1, waiting for transfers between devices, shards(): lax.psum_scatter(grad_qkv_weight.astype(jnp.bfloat16), 'fsdp', scatter_di...  82.7 us
    all_gather x1, waiting for transfers between devices, shards(): lax.all_gather(w_fc, 'fsdp', axis=0, tiled=True)  78.6 us
    unnamed x2, blocking collectives  77.6 us
    all_gather x1, waiting for transfers between devices, shards(): lax.all_gather(w_proj, 'fsdp', axis=0, tiled=True)  74.5 us
    unnamed x13, waiting for transfers between devices  60.2 us
    psum x1, waiting for transfers between devices, shards(): lax.psum(shard_grads[2].astype(jnp.bfloat16), 'ctx').astype(jnp.float32)  37.5 us
  transfers between devices with their start and end apart: 12, of which 11 were waited for; matrix products, arithmetic and copies ran while one was open for 9% of the time, Pallas kernels for 0%

commit v1 on v0

v1 whole, which is shorter than its diff:
```python
import jax
import jax.numpy as jnp
from jax import lax
from jax.experimental import pallas as pl
from jax.experimental.pallas import tpu as pltpu
from jax.sharding import PartitionSpec as P

HEADS = 12
EPS = 1e-05
LOWEST = -1e30
LANES = 128
F32 = jnp.float32
BF16 = jnp.bfloat16
ROW_DOT = (((0,), (0,)), ((), ()))
LANE_DOT = (((1,), (1,)), ((), ()))


def dot(left, right):
    return jnp.dot(left, right, preferred_element_type=F32)


def dot_rows(left, right):
    return lax.dot_general(left, right, ROW_DOT, preferred_element_type=F32)


def dot_lanes(left, right):
    return lax.dot_general(left, right, LANE_DOT, preferred_element_type=F32)


def normalise(values):
    centred = values - jnp.mean(values, axis=-1, keepdims=True)
    spread = jnp.mean(centred * centred, axis=-1, keepdims=True)
    inverse = lax.rsqrt(spread + EPS)
    return centred * inverse, inverse


def norm_backward(incoming, gain, unit, inverse):
    scaled = incoming * gain
    first = jnp.mean(scaled, axis=-1, keepdims=True)
    second = jnp.mean(scaled * unit, axis=-1, keepdims=True)
    return inverse * (scaled - first - unit * second)


def gelu_pair(values):
    inner = 0.7978845608028654 * (values + 0.044715 * values * values * values)
    bent = jnp.tanh(inner)
    slope = 0.7978845608028654 * (1.0 + 0.134145 * values * values)
    value = 0.5 * values * (1.0 + bent)
    derivative = 0.5 * (1.0 + bent) + 0.5 * values * (1.0 - bent * bent) * slope
    return value, derivative


def block_places(block_order, first_row, row_count, block_rows):
    row_index = first_row + jnp.arange(row_count, dtype=jnp.int32)
    which_block = row_index // block_rows
    table = jnp.arange(block_order.shape[0], dtype=jnp.int32)
    picked = jnp.sum(
        jnp.where(which_block[:, None] == table[None, :], block_order[None, :], 0), axis=1
    )
    return picked * block_rows + row_index % block_rows


def attend_kernel(query_place, key_place, q_ref, kv_ref, out_ref, log_ref):
    rows, width = q_ref.shape
    head_dim = width // HEADS
    per_group = LANES // head_dim
    visible = key_place[...] <= query_place[...]
    lane = lax.broadcasted_iota(jnp.int32, (rows, LANES), 1)
    logs = jnp.zeros((rows, LANES), F32)
    for group in range(width // LANES):
        span = pl.ds(group * LANES, LANES)
        q = q_ref[:, span] * (head_dim**-0.5)
        k = kv_ref[:, span]
        v = kv_ref[:, pl.ds(width + group * LANES, LANES)]
        out = jnp.zeros((rows, LANES), F32)
        for part in range(per_group):
            own = lane // head_dim == part
            scores = dot_lanes(jnp.where(own, q, jnp.zeros_like(q)), k)
            scores = jnp.where(visible, scores, LOWEST)
            high = jnp.max(scores, axis=1, keepdims=True)
            shares = jnp.exp(scores - high)
            total = jnp.sum(shares, axis=1, keepdims=True)
            out = jnp.where(own, dot(shares.astype(BF16), v) / total, out)
            logs = jnp.where(lane == group * per_group + part, high + jnp.log(total), logs)
        out_ref[:, span] = out
    log_ref[...] = logs


def attend_back_kernel(
    query_place, key_place, q_ref, kv_ref, att_ref, grad_ref, log_ref, dq_ref, dkv_ref
):
    rows, width = q_ref.shape
    head_dim = width // HEADS
    per_group = LANES // head_dim
    scale = head_dim**-0.5
    visible = key_place[...] <= query_place[...]
    lane = lax.broadcasted_iota(jnp.int32, (rows, LANES), 1)
    for group in range(width // LANES):
        span = pl.ds(group * LANES, LANES)
        far = pl.ds(width + group * LANES, LANES)
        q = q_ref[:, span] * scale
        k = kv_ref[:, span]
        v = kv_ref[:, far]
        grad = grad_ref[:, span]
        product = grad.astype(F32) * att_ref[:, span]
        dq = jnp.zeros((rows, LANES), F32)
        dk = jnp.zeros((k.shape[0], LANES), F32)
        dv = jnp.zeros((k.shape[0], LANES), F32)
        for part in range(per_group):
            own = lane // head_dim == part
            own_q = jnp.where(own, q, jnp.zeros_like(q))
            own_grad = jnp.where(own, grad, jnp.zeros_like(grad))
            delta = jnp.sum(jnp.where(own, product, 0.0), axis=1, keepdims=True)
            log = jnp.sum(
                jnp.where(lane == group * per_group + part, log_ref[...], 0.0),
                axis=1,
                keepdims=True,
            )
            scores = jnp.where(visible, dot_lanes(own_q, k), LOWEST)
            shares = jnp.exp(scores - log)
            dv = dv + dot_rows(shares.astype(BF16), own_grad)
            change = (shares * (dot_lanes(own_grad, v) - delta)).astype(BF16)
            dq = jnp.where(own, dot(change, k) * scale, dq)
            dk = dk + dot_rows(change, own_q)
        dq_ref[:, span] = dq.astype(BF16)
        dkv_ref[:, span] = dk.astype(BF16)
        dkv_ref[:, far] = dv.astype(BF16)


def attend(query_place, key_place, q, kv):
    rows, width = q.shape
    return pl.pallas_call(
        attend_kernel,
        out_shape=(
            jax.ShapeDtypeStruct((rows, width), F32),
            jax.ShapeDtypeStruct((rows, LANES), F32),
        ),
        compiler_params=pltpu.CompilerParams(vmem_limit_bytes=48 * 2**20),
    )(query_place, key_place, q, kv)


def attend_back(query_place, key_place, q, kv, attended, grad, logs):
    return pl.pallas_call(
        attend_back_kernel,
        out_shape=(
            jax.ShapeDtypeStruct(q.shape, BF16),
            jax.ShapeDtypeStruct(kv.shape, BF16),
        ),
        compiler_params=pltpu.CompilerParams(vmem_limit_bytes=48 * 2**20),
    )(query_place, key_place, q, kv, attended, grad, logs)


def shards(
    inputs,
    cotangent,
    block_order,
    norm1_gain,
    norm1_shift,
    w_qkv,
    qv_bias,
    w_out,
    out_bias,
    norm2_gain,
    norm2_shift,
    w_fc,
    fc_bias,
    w_proj,
    proj_bias,
):
    rows, width = inputs.shape[1:]
    positions = lax.axis_size("ctx")
    spread = lax.axis_size("fsdp")
    place = lax.axis_index("ctx")
    core = place % 2
    pairs = [[2 * i, 2 * i + 1] for i in range(positions // 2)]
    lines = [list(range(j, positions, 2)) for j in range(2)]
    shard = width // spread

    def half_of(weight):
        half = weight.shape[1] // 2
        return lax.dynamic_slice_in_dim(weight, core * half, half, 1)

    def gather(weight):
        across = lax.all_gather(weight, "fsdp", axis=0, tiled=True)
        return lax.all_gather(across, "ctx", axis=0, tiled=False, axis_index_groups=pairs)

    def reduce(halves):
        mine = lax.psum_scatter(
            halves, "ctx", scatter_dimension=0, tiled=False, axis_index_groups=pairs
        )
        mine = lax.psum_scatter(mine, "fsdp", scatter_dimension=0, tiled=True)
        mine = lax.psum(mine, "ctx", axis_index_groups=lines)
        return lax.all_gather(mine, "ctx", axis=0, tiled=False, axis_index_groups=pairs)

    def join(halves, begin, end):
        return jnp.concatenate([halves[0][:, begin:end], halves[1][:, begin:end]], axis=1)

    small = jnp.concatenate(
        [
            norm1_gain[None],
            norm1_shift[None],
            qv_bias,
            out_bias[None],
            norm2_gain[None],
            norm2_shift[None],
            proj_bias[None],
            fc_bias.reshape(-1, shard),
        ]
    )
    small = lax.all_gather(small, "fsdp", axis=0).astype(F32)
    vectors = jnp.moveaxis(small[:, :8], 0, 1).reshape(8, width)
    gain_one, shift_one, q_bias, v_bias, out_shift, gain_two, shift_two, proj_shift = vectors
    fc_shift = small[:, 8:].reshape(-1)

    qkv_w = gather(half_of(w_qkv))
    wide = gather(jnp.concatenate([half_of(w_out), half_of(w_fc)], axis=1))
    proj_w = gather(half_of(w_proj))
    out_half = width // 2
    qkv_full = join(qkv_w, 0, qkv_w.shape[2])
    out_full = join(wide, 0, out_half)
    fc_full = join(wide, out_half, wide.shape[2])
    proj_full = join(proj_w, 0, out_half)

    tokens = inputs[0].astype(F32)
    unit_one, inverse_one = normalise(tokens)
    normed_one = (unit_one * gain_one + shift_one).astype(BF16)
    qkv_shift = jnp.concatenate([q_bias, jnp.zeros_like(q_bias), v_bias])
    qkv = (dot(normed_one, qkv_full) + qkv_shift).astype(BF16)
    q = qkv[:, :width]
    kv = lax.all_gather(qkv[:, width:], "ctx", axis=0, tiled=True)
    block_rows = kv.shape[0] // block_order.shape[0]
    query_place = block_places(block_order, place * rows, rows, block_rows)[:, None]
    key_place = block_places(block_order, jnp.int32(0), kv.shape[0], block_rows)[None]
    attended, logs = attend(query_place, key_place, q, kv)
    attended_low = attended.astype(BF16)
    middle = tokens + dot(attended_low, out_full) + out_shift
    unit_two, inverse_two = normalise(middle)
    normed_two = (unit_two * gain_two + shift_two).astype(BF16)
    hidden = dot(normed_two, fc_full) + fc_shift
    activated, slope = gelu_pair(hidden)
    activated = activated.astype(BF16)
    output = middle + dot(activated, proj_full) + proj_shift

    grad_output = cotangent[0]

    def split(left, right):
        half = right.shape[1] // 2
        return jnp.stack(
            [dot_rows(left, right[:, :half]), dot_rows(left, right[:, half:])]
        ).astype(BF16)

    proj_grad = reduce(split(activated, grad_output))
    grad_hidden = (dot_lanes(grad_output, proj_full) * slope).astype(BF16)
    fc_grad = split(normed_two, grad_hidden)
    grad_normed_two = dot_lanes(grad_hidden, fc_full)
    grad_middle = grad_output.astype(F32) + norm_backward(
        grad_normed_two, gain_two, unit_two, inverse_two
    )
    grad_branch = grad_middle.astype(BF16)
    out_grad = split(attended_low, grad_branch)
    wide_grad = reduce(jnp.concatenate([out_grad, fc_grad], axis=2))
    grad_attended = dot_lanes(grad_branch, out_full).astype(BF16)
    dq, dkv = attend_back(query_place, key_place, q, kv, attended, grad_attended, logs)
    dkv = lax.psum_scatter(dkv, "ctx", scatter_dimension=0, tiled=True)
    grad_qkv = jnp.concatenate([dq, dkv], axis=1)
    qkv_grad = reduce(split(normed_one, grad_qkv))
    grad_normed_one = dot_lanes(grad_qkv, qkv_full)
    grad_tokens = grad_middle + norm_backward(grad_normed_one, gain_one, unit_one, inverse_one)

    def total(values):
        return jnp.sum(values, axis=0, dtype=F32)

    columns = total(grad_qkv)
    small_grad = jnp.stack(
        [
            total(grad_normed_one * unit_one),
            total(grad_normed_one),
            columns[:width],
            columns[2 * width :],
            total(grad_branch),
            total(grad_normed_two * unit_two),
            total(grad_normed_two),
            total(grad_output),
        ]
    )
    small_grad = jnp.moveaxis(small_grad.reshape(8, spread, shard), 1, 0)
    small_grad = jnp.concatenate(
        [small_grad, total(grad_hidden).reshape(spread, -1, shard)], axis=1
    )
    small_grad = lax.psum_scatter(small_grad, "fsdp", scatter_dimension=0, tiled=False)
    small_grad = lax.psum(small_grad, "ctx")

    def whole(halves, begin, end):
        return join(halves, begin, end).astype(F32)

    return (
        output[None].astype(BF16),
        grad_tokens[None].astype(BF16),
        small_grad[0],
        small_grad[1],
        whole(qkv_grad, 0, qkv_grad.shape[2]),
        small_grad[2:4],
        whole(wide_grad, 0, out_half),
        small_grad[4],
        small_grad[5],
        small_grad[6],
        whole(wide_grad, out_half, wide_grad.shape[2]),
        small_grad[8:].reshape(-1),
        whole(proj_grad, 0, out_half),
        small_grad[7],
    )


def solution(mesh):
    in_specs = (
        P("fsdp", "ctx", None),
        P("fsdp", "ctx", None),
        P(),
        P("fsdp"),
        P("fsdp"),
        P("fsdp", None),
        P(None, "fsdp"),
        P("fsdp", None),
        P("fsdp"),
        P("fsdp"),
        P("fsdp"),
        P("fsdp", None),
        P("fsdp"),
        P("fsdp", None),
        P("fsdp"),
    )
    out_specs = (
        P("fsdp", "ctx", None),
        P("fsdp", "ctx", None),
        P("fsdp"),
        P("fsdp"),
        P("fsdp", None),
        P(None, "fsdp"),
        P("fsdp", None),
        P("fsdp"),
        P("fsdp"),
        P("fsdp"),
        P("fsdp", None),
        P("fsdp"),
        P("fsdp", None),
        P("fsdp"),
    )
    return jax.shard_map(shards, mesh=mesh, in_specs=in_specs, out_specs=out_specs, check_vma=False)
```

time: 900 us -> 714 us (0.79)
  blocking collectives: 126 us -> 43.4 us
  matrix products: 86 us -> 30.7 us
  waiting for transfers between devices: 585 us -> 548 us
  other arithmetic: 41 us -> 17.9 us
  Pallas kernels: 0 us -> 18.8 us
    unnamed x2 -> x0, blocking collectives: 77.6 us -> none
    unnamed x13 -> x16, waiting for transfers between devices: 60.2 us -> 0.73 us
    dot_general x26 -> x16, matrix products: 86 us -> 30.7 us  [the longest x8 11.8 us: dot_rows(): return lax.dot_general(left, right, ROW_DOT, preferred_element_type=F32)]
    all_gather x5 -> x7, waiting for transfers between devices: 170 us -> 190 us  [the longest x3 160 us: gather(): across = lax.all_gather(weight, 'fsdp', axis=0, tiled=True)]
    pallas_call x0 -> x2, Pallas kernels: none -> 18.8 us  [the longest x1 12.3 us: attend_back(): pl.pallas_call(attend_back_kernel, out_shape=(jax.ShapeDtypeStruct(q.shap...]
    reduce_sum x11 -> x5, other arithmetic: 12.1 us -> 2.06 us  [the longest x2 1.46 us: total(): return jnp.sum(values, axis=0, dtype=F32)]
    reduce_scatter x5 -> x8, waiting for transfers between devices: 317 us -> 327 us  [the longest x3 206 us: reduce(): mine = lax.psum_scatter(mine, 'fsdp', scatter_dimension=0, tiled=True)]
    all_gather x2 -> x4, blocking collectives: 42.5 us -> 37.5 us  [the longest x1 30.4 us: shards(): small = lax.all_gather(small, 'fsdp', axis=0).astype(F32)]
  transfers between devices with their start and end apart: 12 -> 16, of which waited for: 11 -> 13; matrix products, arithmetic and copies ran while one was open for 9% -> 9% of each run, Pallas kernels for 0% -> 0%
where the time goes in v1:
time: 714 us; the launch traced here: 710 us
  waiting for transfers between devices  548 us (77%)
  blocking collectives  43.4 us (6%)
  local copies, waits for them, and re-layouts  35.2 us (5%)
  matrix products  30.7 us (4%)
  Pallas kernels  18.8 us (3%)
  other arithmetic  17.9 us (3%)
  between operations  14.9 us (2%)
    reduce_scatter x3, waiting for transfers between devices, reduce(): mine = lax.psum_scatter(mine, 'fsdp', scatter_dimension=0, tiled=True)  206 us
    all_gather x3, waiting for transfers between devices, gather(): across = lax.all_gather(weight, 'fsdp', axis=0, tiled=True)  160 us
    reduce_scatter x1, waiting for transfers between devices, shards(): lax.psum_scatter(small_grad, 'fsdp', scatter_dimension=0, tiled=False)  63 us
    psum x1, waiting for transfers between devices, reduce(): mine = lax.psum(mine, 'ctx', axis_index_groups=lines)  30.6 us
    all_gather x1, blocking collectives, shards(): small = lax.all_gather(small, 'fsdp', axis=0).astype(F32)  30.4 us
    reduce_scatter x3, waiting for transfers between devices, reduce(): lax.psum_scatter(halves, 'ctx', scatter_dimension=0, tiled=False, axis_in...  29.4 us
    reduce_scatter x1, waiting for transfers between devices, shards(): dkv = lax.psum_scatter(dkv, 'ctx', scatter_dimension=0, tiled=True)  28.4 us
    all_gather x1, waiting for transfers between devices, shards(): kv = lax.all_gather(qkv[:, width:], 'ctx', axis=0, tiled=True)  24.7 us
  transfers between devices with their start and end apart: 16, of which 13 were waited for; matrix products, arithmetic and copies ran while one was open for 9% of the time, Pallas kernels for 0%

profile of v1, /device:TPU:0, one launch (start us, length us, event | category | flops | bytes accessed | tf_op | source)
XLA Modules:
  0.0 710.2 jit_solution(304734693705608641)
XLA Ops:
  7.3 1.7 constant_dynamic-slice_fusion.1
  12.6 46.9 %all-gather.13.cloned.1.call-done = bf16[768,1152]{1,0:T(8,128)(2,1)} async-done(((bf16[96,1152]{1,0:T(8,128)(2,1)}), bf16[768,1152]{1,0:T(8,128)(2,1)}) %all-gather.13.cloned.1.call-update) | async-done | bytes 1769488 | tf_op jit(solution)/shard_map/all_gather | solution.py:184
  59.6 53.7 %all-gather.19.cloned.1.call-done = bf16[3072,384]{1,0:T(8,128)(2,1)} async-done(((bf16[384,384]{1,0:T(8,128)(2,1)}), bf16[3072,384]{1,0:T(8,128)(2,1)}) %all-gather.19.cloned.1.call-update) | async-done | bytes 2359312 | tf_op jit(solution)/shard_map/all_gather | solution.py:184
  113.4 59.6 %all-gather.17.cloned.1.call-done = bf16[768,1920]{1,0:T(8,128)(2,1)} async-done(((bf16[96,1920]{1,0:T(8,128)(2,1)}), bf16[768,1920]{1,0:T(8,128)(2,1)}) %all-gather.17.cloned.1.call-update) | async-done | bytes 2949136 | tf_op jit(solution)/shard_map/all_gather | solution.py:184
  173.3 30.4 %all-gather.4 = bf16[8,12,96]{2,1,0:T(8,128)(2,1)S(1)} all-gather(bf16[1,12,96]{2,1,0:T(8,128)(2,1)S(1)} %bitcast.130), channel_id=2, replica_groups=mesh['fsdp'=8,'ctx'=4] {'fsdp'}, dimensions={0}, use_global_device_ids=true | all-gather | bytes 20736 | tf_op jit(solution)/shard_map/all_gather | solution.py:210
  204.6 2.3 fusion.77
  206.9 1.2 fusion.4
  211.1 5.7 fusion.76
  216.8 4.8 all-gather.23.cloned.1.call-done
  221.6 2.2 fusion.75
  223.8 5.1 fusion.74
  228.9 24.7 %all-gather.15.cloned.1.call-done.kv_ref = bf16[1024,1536]{1,0:T(8,128)(2,1)} async-done(((bf16[256,1536]{1,0:T(8,128)(2,1)}), bf16[1024,1536]{1,0:T(8,128)(2,1)}) %all-gather.15.cloned.1.call-update) | async-done | bytes 3145744 | tf_op jit(solution)/shard_map/all_gather | solution.py:230
  253.5 1.9 copy-done.2
  255.4 6.5 shard_map.254
  261.9 1.6 fusion.79
  263.9 1.5 convolution_add_fusion.1
  266.3 3.2 convert_reduce_fusion
  269.5 1.6 multiply_reduce_fusion
  271.2 1.3 convert_reduce_fusion.4
  273.0 12.3 %shard_map.255 = (bf16[256,768]{1,0:T(8,128)(2,1)S(1)}, bf16[1024,1536]{1,0:T(8,128)(2,1)S(1)}) custom-call(s32[256,1]{1,0:T(8,128)S(1)} %fusion.51.query_place, s32[1,1024]{1,0:T(1,128)S(1)} %fusion.55.key_place, bf16[256,768]{1,0:T(8,128)(2,1)S(1)} %slice.205.q_ref, bf16[1024,1536]{1,0:T(8,128)(2,1)} %all-gather.15.cloned.1.call-done.kv_ref, ...), custom_call_target="tpu_custom_call" | custom-call | tf_op jit(solution)/shard_map/pallas_call | solution.py:143
  285.3 1.7 copy-done.3
  288.0 3.5 fusion.1
  291.5 1.4 fusion.2
  292.9 2.9 pad_maximum_fusion.2
  296.7 28.4 %reduce-scatter.9.cloned.1.call-done = bf16[256,1536]{1,0:T(8,128)(2,1)} async-done(((bf16[1024,1536]{1,0:T(8,128)(2,1)}), bf16[256,1536]{1,0:T(8,128)(2,1)}) %reduce-scatter.9.cloned.1.call-update) | async-done | bytes 786448 | tf_op jit(solution)/shard_map/reduce_scatter | solution.py:264
  325.1 2.1 constant_dynamic-update-slice_fusion
  327.3 1.9 fusion.15
  330.1 2.2 pad_maximum_fusion.4
  333.1 1.1 pad_maximum_fusion.20
  334.2 1.7 copy.35
  336.0 2.4 fusion.13
  339.4 2.9 maximum_maximum_fusion
  343.0 11.9 %reduce-scatter.13.cloned.1.call-done = bf16[1,768,1152]{2,1,0:T(8,128)(2,1)} async-done(((bf16[2,768,1152]{2,1,0:T(8,128)(2,1)}), bf16[1,768,1152]{2,1,0:T(8,128)(2,1)}) %reduce-scatter.13.cloned.1.call-update) | async-done | bytes 1769488 | tf_op jit(solution)/shard_map/reduce_scatter | solution.py:188
  354.9 17.5 %reduce-scatter.17.cloned.1.call-done = bf16[1,768,1920]{2,1,0:T(8,128)(2,1)} async-done(((bf16[2,768,1920]{2,1,0:T(8,128)(2,1)}), bf16[1,768,1920]{2,1,0:T(8,128)(2,1)}) %reduce-scatter.17.cloned.1.call-update) | async-done | bytes 2949136 | tf_op jit(solution)/shard_map/reduce_scatter | solution.py:188
  373.0 3.3 fusion.39
  377.9 6.0 fusion.24
  383.9 62.2 %reduce-scatter.23.cloned.1.call-done = bf16[384,384]{1,0:T(8,128)(2,1)} async-done(((bf16[3072,384]{1,0:T(8,128)(2,1)}), bf16[384,384]{1,0:T(8,128)(2,1)}) %reduce-scatter.23.cloned.1.call-update) | async-done | bytes 294928 | tf_op jit(solution)/shard_map/reduce_scatter | solution.py:191
  446.1 68.4 %reduce-scatter.15.cloned.1.call-done = bf16[96,1152]{1,0:T(8,128)(2,1)} async-done(((bf16[768,1152]{1,0:T(8,128)(2,1)}), bf16[96,1152]{1,0:T(8,128)(2,1)}) %reduce-scatter.15.cloned.1.call-update) | async-done | bytes 221200 | tf_op jit(solution)/shard_map/reduce_scatter | solution.py:191
  514.5 75.1 %reduce-scatter.19.cloned.1.call-done = bf16[96,1920]{1,0:T(8,128)(2,1)} async-done(((bf16[768,1920]{1,0:T(8,128)(2,1)}), bf16[96,1920]{1,0:T(8,128)(2,1)}) %reduce-scatter.19.cloned.1.call-update) | async-done | bytes 368656 | tf_op jit(solution)/shard_map/reduce_scatter | solution.py:191
  589.7 1.1 fusion.45
  590.8 63.0 %reduce-scatter.11.cloned.1.call-done = f32[1,12,96]{2,1,0:T(8,128)} async-done(((f32[8,12,96]{2,1,0:T(8,128)}), f32[1,12,96]{2,1,0:T(8,128)}) %reduce-scatter.11.cloned.1.call-update) | async-done | bytes 4624 | tf_op jit(solution)/shard_map/reduce_scatter | solution.py:290
  653.8 5.9 psum.28
  661.4 30.6 %all-reduce.3.cloned.1.call-done = (bf16[1,96,1152]{2,1,0:T(8,128)(2,1)}, bf16[1,96,1920]{2,1,0:T(8,128)(2,1)}, bf16[1,384,384]{2,1,0:T(8,128)(2,1)}) async-done(((bf16[1,96,1152]{2,1,0:T(8,128)(2,1)}, bf16[1,96,1920]{2,1,0:T(8,128)(2,1)}, bf16[1,384,384]{2,1,0:T(8,128)(2,1)}), (bf16[1,96,1152]{2,1,0:T(8,128)(2,1)}, bf16[1,96,1920]{2,1,0:T(8,128)(2,1)}, ...) | async-done | bytes 884752 | tf_op jit(solution)/shard_map/psum | solution.py:192
  692.0 2.7 all_gather.69
  694.9 2.1 all_gather.67
  697.0 2.4 all_gather.71
  700.4 1.1 maximum_convert_fusion.1
  702.3 1.1 maximum_convert_fusion
  (175 shorter events, 20.3 us)
Async XLA Ops:
  7.2 1.9 copy-start
  7.2 52.3 %all-gather.13.cloned.1.call-start = ((), (), s32[]{:S(2)}) async-start(), calls=%async_computation.8 | async-start | bytes 1990656 | tf_op jit(solution)/shard_map/all_gather | solution.py:184
  9.0 104.4 %all-gather.19.cloned.1.call-start = ((), (), s32[]{:S(2)}) async-start(), calls=%async_computation.11 | async-start | bytes 2654208 | tf_op jit(solution)/shard_map/all_gather | solution.py:184
  9.8 163.2 %all-gather.17.cloned.1.call-start = ((), (), s32[]{:S(2)}) async-start(), calls=%async_computation.10 | async-start | bytes 3317760 | tf_op jit(solution)/shard_map/all_gather | solution.py:184
  12.6 192.0 %all-gather.21.cloned.1.call-start = ((), (), s32[]{:S(2)}) async-start(), calls=%async_computation.20 | async-start | bytes 5308416 | tf_op jit(solution)/shard_map/all_gather | solution.py:185
  59.5 113.7 %copy-start.24 = (bf16[384]{0:T(512)(128)(2,1)S(1)}, bf16[384]{0:T(512)(128)(2,1)}, u32[]{:S(2)}) copy-start(bf16[384]{0:T(512)(128)(2,1)} %param.27) | copy-start | bytes 2308
  59.5 113.7 %copy-start.25 = (bf16[96]{0:T(256)(128)(2,1)S(1)}, bf16[96]{0:T(256)(128)(2,1)}, u32[]{:S(2)}) copy-start(bf16[96]{0:T(256)(128)(2,1)} %param.18) | copy-start | bytes 580
  59.5 113.7 %copy-start.26 = (bf16[96]{0:T(256)(128)(2,1)S(1)}, bf16[96]{0:T(256)(128)(2,1)}, u32[]{:S(2)}) copy-start(bf16[96]{0:T(256)(128)(2,1)} %param.19) | copy-start | bytes 580
  59.5 113.7 %copy-start.27 = (bf16[2,96]{1,0:T(2,128)(2,1)S(1)}, bf16[2,96]{1,0:T(2,128)(2,1)}, u32[]{:S(2)}) copy-start(bf16[2,96]{1,0:T(2,128)(2,1)} %param.21) | copy-start | bytes 1156
  59.5 113.8 %copy-start.28 = (bf16[96]{0:T(256)(128)(2,1)S(1)}, bf16[96]{0:T(256)(128)(2,1)}, u32[]{:S(2)}) copy-start(bf16[96]{0:T(256)(128)(2,1)} %param.23) | copy-start | bytes 580
  59.5 113.8 %copy-start.29 = (bf16[96]{0:T(256)(128)(2,1)S(1)}, bf16[96]{0:T(256)(128)(2,1)}, u32[]{:S(2)}) copy-start(bf16[96]{0:T(256)(128)(2,1)} %param.24) | copy-start | bytes 580
  59.5 113.8 %copy-start.30 = (bf16[96]{0:T(256)(128)(2,1)S(1)}, bf16[96]{0:T(256)(128)(2,1)}, u32[]{:S(2)}) copy-start(bf16[96]{0:T(256)(128)(2,1)} %param.25) | copy-start | bytes 580
  59.5 113.8 %copy-start.31 = (bf16[96]{0:T(256)(128)(2,1)S(1)}, bf16[96]{0:T(256)(128)(2,1)}, u32[]{:S(2)}) copy-start(bf16[96]{0:T(256)(128)(2,1)} %param.29) | copy-start | bytes 580
  59.5 144.6 %copy-start.4 = (bf16[1,256,768]{2,1,0:T(8,128)(2,1)S(1)}, bf16[1,256,768]{2,1,0:T(8,128)(2,1)}, u32[]{:S(2)}) copy-start(bf16[1,256,768]{2,1,0:T(8,128)(2,1)} %param.15) | copy-start | bytes 1179652
  59.5 151.5 %all-gather.25.cloned.1.call-start = ((), (), s32[]{:S(2)}) async-start(), calls=%async_computation.22 | async-start | bytes 7077888 | tf_op jit(solution)/shard_map/all_gather | solution.py:185
  113.4 108.3 %all-gather.23.cloned.1.call-start = ((), (), s32[]{:S(2)}) async-start(), calls=%async_computation.21 | async-start | bytes 8847360 | tf_op jit(solution)/shard_map/all_gather | solution.py:185
  173.1 80.5 %all-gather.15.cloned.1.call-start = ((), (), s32[]{:S(2)}) async-start(), calls=%async_computation.9 | async-start | bytes 3932160 | tf_op jit(solution)/shard_map/all_gather | solution.py:230
  206.9 1.8 copy-start.13
  206.9 3.7 copy-start.23
  209.7 115.5 %reduce-scatter.9.cloned.1.call-start = ((), (), s32[]{:S(2)}) async-start(), calls=%async_computation.12 | async-start | bytes 3932160 | tf_op jit(solution)/shard_map/reduce_scatter | solution.py:264
  223.8 38.1 %copy-start.16 = (bf16[768,384]{1,0:T(8,128)(2,1)}, bf16[768,384]{1,0:T(8,128)(2,1)S(1)}, u32[]{:S(2)}) copy-start(bf16[768,384]{1,0:T(8,128)(2,1)S(1)} %get-tuple-element.46) | copy-start | bytes 1769476
  253.5 1.9 copy-start.2
  255.4 8.4 %copy-start.10 = (bf16[768,1536]{1,0:T(8,128)(2,1)S(1)}, bf16[768,1536]{1,0:T(8,128)(2,1)}, u32[]{:S(2)}) copy-start(bf16[768,1536]{1,0:T(8,128)(2,1)} %get-tuple-element.44) | copy-start | bytes 7077892
  255.4 8.4 %copy-start.11 = (bf16[768,1536]{1,0:T(8,128)(2,1)S(1)}, bf16[768,1536]{1,0:T(8,128)(2,1)}, u32[]{:S(2)}) copy-start(bf16[768,1536]{1,0:T(8,128)(2,1)} %get-tuple-element.45) | copy-start | bytes 7077892
  263.8 1.7 copy-start.8
  263.8 2.4 copy-start.9
  263.8 2.4 copy-start.19
  265.3 4.2 copy-start.32
  269.5 1.6 copy-start.14
  271.1 1.3 copy-start.17
  271.2 1.3 copy-start.18
  285.2 1.8 copy-start.3
  287.0 55.4 %reduce-scatter.21.cloned.1.call-start = ((), (), s32[]{:S(2)}) async-start(), calls=%async_computation.18 | async-start | bytes 7077888 | tf_op jit(solution)/shard_map/reduce_scatter | solution.py:188
  288.0 3.5 copy-start.33
  295.9 59.0 %reduce-scatter.13.cloned.1.call-start = ((), (), s32[]{:S(2)}) async-start(), calls=%async_computation.14 | async-start | bytes 5308416 | tf_op jit(solution)/shard_map/reduce_scatter | solution.py:188
  325.1 4.1 copy-start.7
  332.3 40.1 %reduce-scatter.17.cloned.1.call-start = ((), (), s32[]{:S(2)}) async-start(), calls=%async_computation.16 | async-start | bytes 8847360 | tf_op jit(solution)/shard_map/reduce_scatter | solution.py:188
  335.9 2.4 copy-start.15
  342.3 103.8 %reduce-scatter.23.cloned.1.call-start = ((), (), s32[]{:S(2)}) async-start(), calls=%async_computation.19 | async-start | bytes 2654208 | tf_op jit(solution)/shard_map/reduce_scatter | solution.py:191
  342.4 30.6 %copy-start.5 = (bf16[256,2304]{1,0:T(8,128)(2,1)S(1)}, bf16[256,2304]{1,0:T(8,128)(2,1)}, u32[]{:S(2)}) copy-start(bf16[256,2304]{1,0:T(8,128)(2,1)} %constant_dynamic-update-slice_fusion) | copy-start | bytes 3538948
  342.9 171.6 %reduce-scatter.15.cloned.1.call-start = ((), (), s32[]{:S(2)}) async-start(), calls=%async_computation.15 | async-start | bytes 1990656 | tf_op jit(solution)/shard_map/reduce_scatter | solution.py:191
  354.9 234.7 %reduce-scatter.19.cloned.1.call-start = ((), (), s32[]{:S(2)}) async-start(), calls=%async_computation.17 | async-start | bytes 3317760 | tf_op jit(solution)/shard_map/reduce_scatter | solution.py:191
  372.4 281.3 %reduce-scatter.11.cloned.1.call-start = ((), (), s32[]{:S(2)}) async-start(), calls=%async_computation.13 | async-start | bytes 73728 | tf_op jit(solution)/shard_map/reduce_scatter | solution.py:290
  377.5 212.2 %copy-start.6 = (f32[256,768]{1,0:T(8,128)S(1)}, f32[256,768]{1,0:T(8,128)}, u32[]{:S(2)}) copy-start(f32[256,768]{1,0:T(8,128)} %get-tuple-element.43) | copy-start | bytes 2359300
  377.5 314.5 %all-reduce.3.cloned.1.call-start = ((), (), s32[]{:S(2)}) async-start(), calls=%async_computation.23 | async-start | bytes 1769472 | tf_op jit(solution)/shard_map/psum | solution.py:192
  692.0 2.8 copy-start.22
  692.0 5.0 copy-start.21
  697.0 6.4 copy-start.1
  (2 other events, 2.3 us)
Sparse Core Ops, SparseCore 0:
  10.8 48.6 all-gather.12
  62.2 51.0 all-gather.18
  116.1 56.8 all-gather.16
  174.4 11.3 all-gather.20
  187.2 15.5 all-gather.24
  204.2 17.3 all-gather.22
  223.7 29.7 all-gather.14
  287.1 37.9 reduce-scatter.8
  327.5 12.6 reduce-scatter.20
  342.3 12.5 reduce-scatter.12
  357.3 15.0 reduce-scatter.16
  375.8 70.2 reduce-scatter.22
  449.6 64.8 reduce-scatter.14
  518.3 71.2 reduce-scatter.18
  593.5 60.2 reduce-scatter.10
  656.1 35.8 all-reduce.2

commit v2 on v1

--- a/solution.py
+++ b/solution.py
@@ -1,3 +1,5 @@
+from functools import partial
+
 import jax
 import jax.numpy as jnp
 from jax import lax
@@ -149,6 +151,258 @@
         compiler_params=pltpu.CompilerParams(vmem_limit_bytes=48 * 2**20),
     )(query_place, key_place, q, kv, attended, grad, logs)
 
+MESH = pl.DeviceIdType.MESH
+GATHER_ID = 0
+REDUCE_ID = 1
+
+
+def ring_order(fsdp, depth):
+    across = fsdp // depth
+    order = []
+    for z in range(depth):
+        columns = list(range(1, across))
+        order += [z * across + y for y in (columns if z % 2 == 0 else columns[::-1])]
+    return order + [z * across for z in range(depth - 1, -1, -1)]
+
+
+def pick(table, index):
+    found = jnp.int32(table[0])
+    for at in range(1, len(table)):
+        found = jnp.where(index == at, jnp.int32(table[at]), found)
+    return found
+
+
+def ring_blocks(order, position):
+    size = len(order)
+    return [pick(order, lax.rem(position + shift, size)) for shift in range(size)]
+
+
+def remote(source, target, send, receive, device):
+    return pltpu.make_async_remote_copy(
+        src_ref=source,
+        dst_ref=target,
+        send_sem=send,
+        recv_sem=receive,
+        device_id=device,
+        device_id_type=MESH,
+    )
+
+
+def greet(devices):
+    barrier = pltpu.get_barrier_semaphore()
+    for device in devices:
+        pl.semaphore_signal(barrier, inc=1, device_id=device, device_id_type=MESH)
+    pl.semaphore_wait(barrier, len(devices))
+
+
+def gather_kernel(order, count, *refs):
+    ins, outs = refs[:count], refs[count : 2 * count]
+    send, receive, pair_send, pair_receive, local = refs[2 * count :]
+    size = len(order)
+    me, ctx = lax.axis_index("fsdp"), lax.axis_index("ctx")
+    core = lax.rem(ctx, 2)
+    sibling = (me, ctx + 1 - 2 * core)
+    inverse = [order.index(at) for at in range(size)]
+    block = ring_blocks(order, pick(inverse, me))
+    following, preceding = (block[1], ctx), (block[size - 1], ctx)
+    greet([following, preceding, sibling])
+    started = []
+    for a in range(count):
+        copy = pltpu.make_async_copy(ins[a].at[core], outs[a].at[me, core], local.at[a])
+        copy.start()
+        started.append(copy)
+    pending = []
+    hops = [(size // 2, size - 1 - size // 2), (size - 1 - size // 2, size // 2)]
+    for step in range(size // 2 + 1):
+        for a in range(count):
+            for way in range(2):
+                total = hops[a % 2][way]
+                shift = (size - step) % size if way == 0 else step
+                at = block[shift]
+                source = outs[a].at[at, core] if step else ins[a].at[core]
+                if 0 < step <= total:
+                    remote(
+                        source, source, send.at[a, way, step - 1],
+                        receive.at[a, way, step - 1], following,
+                    ).wait_recv()
+                if step < total:
+                    copy = remote(
+                        source, outs[a].at[at, core], send.at[a, way, step],
+                        receive.at[a, way, step], following if way == 0 else preceding,
+                    )
+                    copy.start()
+                    pending.append(copy)
+                if 0 < step <= total or (step == 0 and way == 0):
+                    copy = remote(
+                        source, outs[a].at[at, core], pair_send.at[a, shift],
+                        pair_receive.at[a, shift], sibling,
+                    )
+                    copy.start()
+                    pending.append(copy)
+    for a in range(count):
+        for shift in range(size):
+            target = outs[a].at[block[shift], 1 - core]
+            remote(
+                target, target, pair_send.at[a, shift], pair_receive.at[a, shift], sibling
+            ).wait_recv()
+    for copy in pending:
+        copy.wait_send()
+    for copy in started:
+        copy.wait()
+
+
+def gather_all(shards, order):
+    count, size = len(shards), len(order)
+    dma = pltpu.SemaphoreType.DMA
+    return pl.pallas_call(
+        partial(gather_kernel, order, count),
+        out_shape=[jax.ShapeDtypeStruct((size,) + s.shape, s.dtype) for s in shards],
+        in_specs=[pl.BlockSpec(memory_space=pl.ANY)] * count,
+        out_specs=[pl.BlockSpec(memory_space=pl.ANY)] * count,
+        scratch_shapes=[
+            dma((count, 2, size // 2)),
+            dma((count, 2, size // 2)),
+            dma((count, size)),
+            dma((count, size)),
+            dma((count,)),
+        ],
+        compiler_params=pltpu.CompilerParams(collective_id=GATHER_ID, has_side_effects=True),
+    )(*shards)
+
+
+def reduce_kernel(order, lines, count, *refs):
+    ins, outs = refs[:count], refs[count : 2 * count]
+    pairs = refs[2 * count : 3 * count]
+    slots = refs[3 * count : 4 * count]
+    crossed = refs[4 * count : 5 * count]
+    ring_send, ring_receive, pair_send, pair_receive = refs[5 * count : 5 * count + 4]
+    line_send, line_receive, last_send, last_receive = refs[5 * count + 4 :]
+    size = len(order)
+    me, ctx = lax.axis_index("fsdp"), lax.axis_index("ctx")
+    core = lax.rem(ctx, 2)
+    line = ctx // 2
+    sibling = (me, ctx + 1 - 2 * core)
+    inverse = [order.index(at) for at in range(size)]
+    block = ring_blocks(order, pick(inverse, me))
+    ways = [(block[1], ctx), (block[size - 1], ctx)]
+    peers = [(me, lax.rem(line + k, lines) * 2 + core) for k in range(1, lines)]
+    greet(ways + [sibling] + peers)
+    pending = []
+
+    def shift_of(way, step):
+        return (size - 1 - step) % size if way == 0 else (1 + step) % size
+
+    ready = []
+    for step in range(size):
+        for way in range(2):
+            shift = shift_of(way, step)
+            if shift not in ready:
+                ready.append(shift)
+                for a in range(count):
+                    copy = remote(
+                        ins[a].at[block[shift], 1 - core], pairs[a].at[block[shift]],
+                        pair_send.at[a, shift], pair_receive.at[a, shift], sibling,
+                    )
+                    copy.start()
+                    pending.append(copy)
+    waited = []
+
+    def arrive(shift):
+        if shift not in waited:
+            waited.append(shift)
+            for a in range(count):
+                target = pairs[a].at[block[shift]]
+                remote(
+                    target, target, pair_send.at[a, shift], pair_receive.at[a, shift], sibling
+                ).wait_recv()
+
+    for step in range(size):
+        for way in range(2):
+            shift = shift_of(way, step)
+            arrive(shift)
+            at = block[shift]
+            for a in range(count):
+                half = ins[a].shape[3] // 2
+                span = pl.ds(way * half, half)
+                value = ins[a][at, core, :, span].astype(F32) + pairs[a][at, :, span].astype(F32)
+                if step:
+                    slot = slots[a].at[way, step - 1]
+                    remote(
+                        slot, slot, ring_send.at[a, way, step - 1],
+                        ring_receive.at[a, way, step - 1], ways[way],
+                    ).wait_recv()
+                    value = value + slot[...].astype(F32)
+                if step < size - 1:
+                    held = slots[a].at[way, step - 1 if step else size - 1]
+                    held[...] = value.astype(BF16)
+                    copy = remote(
+                        held, slots[a].at[way, step], ring_send.at[a, way, step],
+                        ring_receive.at[a, way, step], ways[way],
+                    )
+                    copy.start()
+                    pending.append(copy)
+                else:
+                    crossed[a][line, :, span] = value.astype(BF16)
+    for a in range(count):
+        for k in range(1, lines):
+            copy = remote(
+                crossed[a].at[line], crossed[a].at[line], line_send.at[a, k - 1],
+                line_receive.at[a, k - 1], peers[k - 1],
+            )
+            copy.start()
+            pending.append(copy)
+    for a in range(count):
+        for k in range(1, lines):
+            target = crossed[a].at[lax.rem(line + lines - k, lines)]
+            remote(
+                target, target, line_send.at[a, k - 1], line_receive.at[a, k - 1], peers[k - 1]
+            ).wait_recv()
+        value = crossed[a][0].astype(F32)
+        for k in range(1, lines):
+            value = value + crossed[a][k].astype(F32)
+        outs[a][core] = value.astype(BF16)
+        copy = remote(
+            outs[a].at[core], outs[a].at[core], last_send.at[a], last_receive.at[a], sibling
+        )
+        copy.start()
+        pending.append(copy)
+    for a in range(count):
+        target = outs[a].at[1 - core]
+        remote(target, target, last_send.at[a], last_receive.at[a], sibling).wait_recv()
+    for copy in pending:
+        copy.wait_send()
+
+
+def reduce_all(grads, order, lines):
+    count, size = len(grads), len(order)
+    dma = pltpu.SemaphoreType.DMA
+    vmem = pl.BlockSpec(memory_space=pltpu.VMEM)
+    scratch = [pltpu.VMEM((size,) + g.shape[2:], BF16) for g in grads]
+    scratch += [pltpu.VMEM((2, size, g.shape[2], g.shape[3] // 2), BF16) for g in grads]
+    scratch += [pltpu.VMEM((lines,) + g.shape[2:], BF16) for g in grads]
+    scratch += [dma((count, 2, size - 1)), dma((count, 2, size - 1))]
+    scratch += [dma((count, size)), dma((count, size))]
+    scratch += [dma((count, max(lines - 1, 1))), dma((count, max(lines - 1, 1)))]
+    scratch += [dma((count,)), dma((count,))]
+    return pl.pallas_call(
+        partial(reduce_kernel, order, lines, count),
+        out_shape=[jax.ShapeDtypeStruct(g.shape[1:], BF16) for g in grads],
+        in_specs=[vmem] * count,
+        out_specs=[vmem] * count,
+        scratch_shapes=scratch,
+        compiler_params=pltpu.CompilerParams(
+            collective_id=REDUCE_ID, has_side_effects=True, vmem_limit_bytes=56 * 2**20
+        ),
+    )(*grads)
+
+
+def round_up(value, unit):
+    return -(-value // unit) * unit
+
+
+def pad_to(array, shape):
+    return jnp.pad(array, [(0, new - old) for old, new in zip(array.shape, shape)])
+
 
 def shards(
     inputs,
@@ -171,29 +425,28 @@
     positions = lax.axis_size("ctx")
     spread = lax.axis_size("fsdp")
     place = lax.axis_index("ctx")
-    core = place % 2
-    pairs = [[2 * i, 2 * i + 1] for i in range(positions // 2)]
-    lines = [list(range(j, positions, 2)) for j in range(2)]
+    lines = positions // 2
+    order = ring_order(spread, spread // lines if spread % lines == 0 else spread // 2)
     shard = width // spread
-
-    def half_of(weight):
-        half = weight.shape[1] // 2
-        return lax.dynamic_slice_in_dim(weight, core * half, half, 1)
-
-    def gather(weight):
-        across = lax.all_gather(weight, "fsdp", axis=0, tiled=True)
-        return lax.all_gather(across, "ctx", axis=0, tiled=False, axis_index_groups=pairs)
-
-    def reduce(halves):
-        mine = lax.psum_scatter(
-            halves, "ctx", scatter_dimension=0, tiled=False, axis_index_groups=pairs
-        )
-        mine = lax.psum_scatter(mine, "fsdp", scatter_dimension=0, tiled=True)
-        mine = lax.psum(mine, "ctx", axis_index_groups=lines)
-        return lax.all_gather(mine, "ctx", axis=0, tiled=False, axis_index_groups=pairs)
-
-    def join(halves, begin, end):
-        return jnp.concatenate([halves[0][:, begin:end], halves[1][:, begin:end]], axis=1)
+    sixteen = 16
+
+    def two(weight):
+        part = weight.shape[0] // 2
+        weight = weight.reshape(2, part, weight.shape[1])
+        return pad_to(weight, (2, round_up(part, sixteen), weight.shape[2]))
+
+    def full(gathered, weight):
+        part = weight.shape[0] // 2
+        return gathered[:, :, :part].reshape(-1, weight.shape[1])
+
+    def spread_out(grad):
+        part = grad.shape[0] // spread // 2
+        grad = grad.astype(BF16).reshape(spread, 2, part, grad.shape[1])
+        return pad_to(grad, (spread, 2, round_up(part, sixteen), grad.shape[3]))
+
+    def own(reduced, weight):
+        part = weight.shape[0] // 2
+        return reduced[:, :part].reshape(weight.shape).astype(F32)
 
     small = jnp.concatenate(
         [
@@ -207,19 +460,19 @@
             fc_bias.reshape(-1, shard),
         ]
     )
-    small = lax.all_gather(small, "fsdp", axis=0).astype(F32)
+    small_rows = small.shape[0]
+    small = pad_to(small, (2 * sixteen, round_up(shard, LANES))).reshape(2, sixteen, -1)
+    qkv_full, fc_full, out_full, proj_full, small = gather_all(
+        [two(w_qkv), two(w_fc), two(w_out), two(w_proj), small], order
+    )
+    qkv_full = full(qkv_full, w_qkv)
+    fc_full = full(fc_full, w_fc)
+    out_full = full(out_full, w_out)
+    proj_full = full(proj_full, w_proj)
+    small = small.reshape(spread, 2 * sixteen, -1)[:, :small_rows, :shard].astype(F32)
     vectors = jnp.moveaxis(small[:, :8], 0, 1).reshape(8, width)
     gain_one, shift_one, q_bias, v_bias, out_shift, gain_two, shift_two, proj_shift = vectors
     fc_shift = small[:, 8:].reshape(-1)
-
-    qkv_w = gather(half_of(w_qkv))
-    wide = gather(jnp.concatenate([half_of(w_out), half_of(w_fc)], axis=1))
-    proj_w = gather(half_of(w_proj))
-    out_half = width // 2
-    qkv_full = join(qkv_w, 0, qkv_w.shape[2])
-    out_full = join(wide, 0, out_half)
-    fc_full = join(wide, out_half, wide.shape[2])
-    proj_full = join(proj_w, 0, out_half)
 
     tokens = inputs[0].astype(F32)
     unit_one, inverse_one = normalise(tokens)
@@ -243,27 +496,20 @@
 
     grad_output = cotangent[0]
 
-    def split(left, right):
-        half = right.shape[1] // 2
-        return jnp.stack(
-            [dot_rows(left, right[:, :half]), dot_rows(left, right[:, half:])]
-        ).astype(BF16)
-
-    proj_grad = reduce(split(activated, grad_output))
+    proj_grad = dot_rows(activated, grad_output)
     grad_hidden = (dot_lanes(grad_output, proj_full) * slope).astype(BF16)
-    fc_grad = split(normed_two, grad_hidden)
+    fc_grad = dot_rows(normed_two, grad_hidden)
     grad_normed_two = dot_lanes(grad_hidden, fc_full)
     grad_middle = grad_output.astype(F32) + norm_backward(
         grad_normed_two, gain_two, unit_two, inverse_two
     )
     grad_branch = grad_middle.astype(BF16)
-    out_grad = split(attended_low, grad_branch)
-    wide_grad = reduce(jnp.concatenate([out_grad, fc_grad], axis=2))
+    out_grad = dot_rows(attended_low, grad_branch)
     grad_attended = dot_lanes(grad_branch, out_full).astype(BF16)
     dq, dkv = attend_back(query_place, key_place, q, kv, attended, grad_attended, logs)
     dkv = lax.psum_scatter(dkv, "ctx", scatter_dimension=0, tiled=True)
     grad_qkv = jnp.concatenate([dq, dkv], axis=1)
-    qkv_grad = reduce(split(normed_one, grad_qkv))
+    qkv_grad = dot_rows(normed_one, grad_qkv)
     grad_normed_one = dot_lanes(grad_qkv, qkv_full)
     grad_tokens = grad_middle + norm_backward(grad_normed_one, gain_one, unit_one, inverse_one)
 
@@ -287,26 +533,36 @@
     small_grad = jnp.concatenate(
         [small_grad, total(grad_hidden).reshape(spread, -1, shard)], axis=1
     )
-    small_grad = lax.psum_scatter(small_grad, "fsdp", scatter_dimension=0, tiled=False)
-    small_grad = lax.psum(small_grad, "ctx")
-
-    def whole(halves, begin, end):
-        return join(halves, begin, end).astype(F32)
+    small_grad = pad_to(
+        small_grad, (spread, 2 * sixteen, round_up(shard, 2 * LANES))
+    ).reshape(spread, 2, sixteen, -1)
+    qkv_grad, fc_grad, out_grad, proj_grad, small_grad = reduce_all(
+        [
+            spread_out(qkv_grad),
+            spread_out(fc_grad),
+            spread_out(out_grad),
+            spread_out(proj_grad),
+            small_grad.astype(BF16),
+        ],
+        order,
+        lines,
+    )
+    small_grad = small_grad.reshape(2 * sixteen, -1)[:small_rows, :shard].astype(F32)
 
     return (
         output[None].astype(BF16),
         grad_tokens[None].astype(BF16),
         small_grad[0],
         small_grad[1],
-        whole(qkv_grad, 0, qkv_grad.shape[2]),
+        own(qkv_grad, w_qkv),
         small_grad[2:4],
-        whole(wide_grad, 0, out_half),
+        own(out_grad, w_out),
         small_grad[4],
         small_grad[5],
         small_grad[6],
-        whole(wide_grad, out_half, wide_grad.shape[2]),
+        own(fc_grad, w_fc),
         small_grad[8:].reshape(-1),
-        whole(proj_grad, 0, out_half),
+        own(proj_grad, w_proj),
         small_grad[7],
     )
 

time: 714 us -> 332 us (0.46)
  waiting for transfers between devices: 548 us -> 50.9 us
  Pallas kernels: 18.8 us -> 202 us
  blocking collectives: 43.4 us -> 0 us
  local copies, waits for them, and re-layouts: 35.2 us -> 15.6 us
    reduce_scatter x7 -> x0, waiting for transfers between devices: 298 us -> none  [the longest x3 206 us: reduce(): mine = lax.psum_scatter(mine, 'fsdp', scatter_dimension=0, tiled=True)]
    pallas_call x0 -> x2, Pallas kernels: none -> 183 us  [the longest x1 105 us: reduce_all(): pl.pallas_call(partial(reduce_kernel, order, lines, count), out_shape=[ja...]
    all_gather x6 -> x0, waiting for transfers between devices: 165 us -> none  [the longest x3 160 us: gather(): across = lax.all_gather(weight, 'fsdp', axis=0, tiled=True)]
    all_gather x4 -> x0, blocking collectives: 37.5 us -> none  [the longest x1 30.4 us: shards(): small = lax.all_gather(small, 'fsdp', axis=0).astype(F32)]
    psum x1 -> x0, waiting for transfers between devices: 30.6 us -> none  [reduce(): mine = lax.psum(mine, 'ctx', axis_index_groups=lines)]
    slice x8 -> x0, local copies, waits for them, and re-layouts: 15.3 us -> none  [the longest x6 15.3 us: join(): halves[0][:, begin:end]]
  transfers between devices with their start and end apart: 16 -> 2, of which waited for: 13 -> 2; matrix products, arithmetic and copies ran while one was open for 9% -> 5% of each run, Pallas kernels for 0% -> 0%
where the time goes in v2:
time: 332 us; the launch traced here: 329 us
  Pallas kernels  202 us (61%)
  waiting for transfers between devices  50.9 us (15%)
  matrix products  32 us (10%)
  local copies, waits for them, and re-layouts  15.6 us (5%)
  between operations  14.6 us (4%)
  other arithmetic  13.1 us (4%)
    pallas_call x1, Pallas kernels, reduce_all(): pl.pallas_call(partial(reduce_kernel, order, lines, count), out_shape=[ja...  105 us
    pallas_call x1, Pallas kernels, gather_all(): pl.pallas_call(partial(gather_kernel, order, count), out_shape=[jax.Shape...  78.1 us
    all_gather x1, waiting for transfers between devices, shards(): kv = lax.all_gather(qkv[:, width:], 'ctx', axis=0, tiled=True)  28 us
    reduce_scatter x1, waiting for transfers between devices, shards(): dkv = lax.psum_scatter(dkv, 'ctx', scatter_dimension=0, tiled=True)  22.9 us
    dot_general x4, matrix products, dot_rows(): return lax.dot_general(left, right, ROW_DOT, preferred_element_type=F32)  14.2 us
    pallas_call x1, Pallas kernels, attend_back(): pl.pallas_call(attend_back_kernel, out_shape=(jax.ShapeDtypeStruct(q.shap...  12.5 us
    dot_general x4, matrix products, dot(): return jnp.dot(left, right, preferred_element_type=F32)  9.33 us
    dot_general x4, matrix products, dot_lanes(): return lax.dot_general(left, right, LANE_DOT, preferred_element_type=F32)  8.47 us
  transfers between devices with their start and end apart: 2, of which 2 were waited for; matrix products, arithmetic and copies ran while one was open for 5% of the time, Pallas kernels for 0%

profile of v2, /device:TPU:0, one launch (start us, length us, event | category | flops | bytes accessed | tf_op | source)
XLA Modules:
  0.0 328.6 jit_solution(4758492003188003400)
XLA Ops:
  7.2 0.8 reshape.344
  8.0 0.8 concatenate.15
  8.8 0.6 pad.9
  9.4 78.1 %shard_map.254 = (bf16[8,2,48,2304]{3,2,1,0:T(8,128)(2,1)}, bf16[8,2,48,3072]{3,2,1,0:T(8,128)(2,1)}, bf16[8,2,48,768]{3,2,1,0:T(8,128)(2,1)}, bf16[8,2,192,768]{3,2,1,0:T(8,128)(2,1)}, bf16[8,2,16,128]{3,2,1,0:T(8,128)(2,1)}) custom-call(bf16[2,48,2304]{2,1,0:T(8,128)(2,1)} %bitcast.133, bf16[2,48,3072]{2,1,0:T(8,128)(2,1)} %bitcast.130, ...), custom_call_target="tpu_custom_call" | custom-call | tf_op jit(solution)/shard_map/pallas_call | solution.py:257
  87.5 0.8 slice_convert_fusion
  88.7 1.1 convert_reduce_fusion
  89.8 1.2 fusion.28
  91.1 3.3 %fusion.2 = bf16[256,2304]{1,0:T(8,128)(2,1)S(1)} fusion(bf16[768,2304]{1,0:T(8,128)(2,1)} %bitcast.155, f32[2304]{0:T(1024)S(1)} %pad_maximum_fusion.1, bf16[1,256,768]{2,1,0:T(8,128)(2,1)} %param.15, f32[768]{0:T(1024)S(1)} %add.195, f32[768]{0:T(1024)S(1)} %mul.192, f32[256]{0:T(256)S(1)} %add_rsqrt_fusion.1, f32[256]{0:T(256)S(1)} %broadcast_multiply_fusion.6), kind=kOutput, calls=%fused_computation.10 | convolution fusion | flops 908328960 | bytes 5129216 | tf_op jit(solution)/shard_map/dot_general | solution.py:21
  94.4 0.9 slice.89
  95.4 0.2 reduce-scatter.2.cloned.1.call-start
  95.9 0.1 copy.34
  96.4 28.0 %all-gather.2.cloned.1.call-done.kv_ref = bf16[1024,1536]{1,0:T(8,128)(2,1)} async-done(((bf16[256,1536]{1,0:T(8,128)(2,1)}), bf16[1024,1536]{1,0:T(8,128)(2,1)}) %all-gather.2.cloned.1.call-update) | async-done | bytes 3145744 | tf_op jit(solution)/shard_map/all_gather | solution.py:483
  124.4 1.9 copy-done
  126.3 6.5 %shard_map.255 = (f32[256,768]{1,0:T(8,128)S(1)}, f32[256,128]{1,0:T(8,128)S(1)}) custom-call(s32[256,1]{1,0:T(8,128)S(1)} %fusion.50.query_place, s32[1,1024]{1,0:T(1,128)S(1)} %fusion.54.key_place, bf16[256,768]{1,0:T(8,128)(2,1)S(1)} %slice.88.q_ref, bf16[1024,1536]{1,0:T(8,128)(2,1)S(1)} %copy-done), custom_call_target="tpu_custom_call" | custom-call | tf_op jit(solution)/shard_map/pallas_call | solution.py:134
  132.8 1.8 fusion.61
  134.7 0.2 multiply_reduce_fusion.2
  134.9 1.5 convolution_add_fusion.1
  136.4 0.4 slice-done
  137.0 0.2 slice-done.1
  137.1 3.0 fusion.62
  140.2 1.1 copy-done.8
  141.3 1.7 multiply_reduce_fusion
  143.0 0.3 convert_reduce_fusion.1
  143.4 0.9 copy-done.6
  144.3 0.5 convolution_convert_fusion.4.grad_ref
  144.8 12.5 %shard_map.256 = (bf16[256,768]{1,0:T(8,128)(2,1)S(1)}, bf16[1024,1536]{1,0:T(8,128)(2,1)S(1)}) custom-call(s32[256,1]{1,0:T(8,128)S(1)} %fusion.50.query_place, s32[1,1024]{1,0:T(1,128)S(1)} %fusion.54.key_place, bf16[256,768]{1,0:T(8,128)(2,1)S(1)} %slice.88.q_ref, bf16[1024,1536]{1,0:T(8,128)(2,1)} %all-gather.2.cloned.1.call-done.kv_ref, ...), custom_call_target="tpu_custom_call" | custom-call | tf_op jit(solution)/shard_map/pallas_call | solution.py:145
  157.3 1.6 copy-done.1
  159.5 0.8 constant_dynamic-update-slice_fusion.1
  160.3 2.7 convolution_convert_fusion.3
  163.0 4.1 %convolution_convert_fusion.1 = bf16[768,3072]{1,0:T(8,128)(2,1)} fusion(bf16[256,3072]{1,0:T(8,128)(2,1)S(1)} %copy-done.9, f32[256,768]{1,0:T(8,128)S(1)} %get-tuple-element.69, f32[768]{0:T(1024)S(1)} %add.205, f32[768]{0:T(1024)S(1)} %mul.198, f32[256]{0:T(256)S(1)} %add_rsqrt_fusion, f32[256]{0:T(256)S(1)} %broadcast_multiply_fusion.5), kind=kOutput, calls=%fused_computation.1 | convolution fusion | flops 1211301888 | bytes 7086080 | tf_op jit(solution)/shard_map/dot_general | solution.py:25
  167.1 4.4 %convolution_convert_fusion = bf16[3072,768]{1,0:T(8,128)(2,1)} fusion(bf16[1,256,768]{2,1,0:T(8,128)(2,1)S(1)} %copy-done.7, f32[256,3072]{1,0:T(8,128)S(1)} %copy-done.14), kind=kOutput, calls=%fused_computation | convolution fusion | flops 1217396736 | bytes 8257536 | tf_op jit(solution)/shard_map/dot_general | solution.py:25
  171.5 2.7 fusion.12
  174.2 22.9 %reduce-scatter.2.cloned.1.call-done = bf16[256,1536]{1,0:T(8,128)(2,1)} async-done(((bf16[1024,1536]{1,0:T(8,128)(2,1)}), bf16[256,1536]{1,0:T(8,128)(2,1)}) %reduce-scatter.2.cloned.1.call-update) | async-done | bytes 786448 | tf_op jit(solution)/shard_map/reduce_scatter | solution.py:510
  197.1 1.2 constant_dynamic-update-slice_fusion
  198.3 3.3 %fusion.27 = (bf16[768]{0:T(1024)(128)(2,1)S(1)}, f32[256]{0:T(256)S(1)}, f32[256]{0:T(256)S(1)}, bf16[768]{0:T(1024)(128)(2,1)S(1)}, f32[256,768]{1,0:T(8,128)S(1)}) fusion(bf16[1,256,768]{2,1,0:T(8,128)(2,1)S(1)} %copy-done.2, f32[256]{0:T(256)S(1)} %add_rsqrt_fusion.1, f32[256]{0:T(256)S(1)} %broadcast_multiply_fusion.6, f32[768]{0:T(1024)S(1)} %mul.192, ...), kind=kOutput, calls=%fused_computation.43 | convolution fusion | flops 907933696 | bytes 5908480 | tf_op jit(solution)/shard_map/dot_general | solution.py:29
  201.6 3.0 convolution_convert_fusion.2
  204.6 0.2 reduce.1
  205.3 0.7 pad.10.clone
  205.9 105.1 %shard_map.257 = (bf16[2,48,2304]{2,1,0:T(8,128)(2,1)}, bf16[2,48,3072]{2,1,0:T(8,128)(2,1)}, bf16[2,48,768]{2,1,0:T(8,128)(2,1)}, bf16[2,192,768]{2,1,0:T(8,128)(2,1)}, bf16[2,16,256]{2,1,0:T(8,128)(2,1)}) custom-call(bf16[8,2,48,2304]{3,2,1,0:T(8,128)(2,1)} %bitcast.125, bf16[8,2,48,3072]{3,2,1,0:T(8,128)(2,1)} %bitcast.124, ...), custom_call_target="tpu_custom_call" | custom-call | tf_op jit(solution)/shard_map/pallas_call | solution.py:387
  311.1 0.8 slice_convert_fusion.1
  311.8 0.5 slice_bitcast_fusion.1
  312.4 0.6 slice.96
  313.0 2.0 bitcast_convert_fusion.2
  314.9 1.6 bitcast_convert_fusion.3
  316.6 2.2 bitcast_convert_fusion.1
  318.8 0.7 reshape.357
  319.4 1.1 bitcast_convert_fusion
  320.6 1.1 fusion.36
  (90 shorter events, 2.3 us)
Async XLA Ops:
  7.2 117.3 %all-gather.2.cloned.1.call-start = ((), (), s32[]{:S(2)}) async-start(), calls=%async_computation.1 | async-start | bytes 3932160 | tf_op jit(solution)/shard_map/all_gather | solution.py:483
  94.4 1.3 copy-start.11
  95.4 37.4 %copy-start.2 = (bf16[1,256,768]{2,1,0:T(8,128)(2,1)S(1)}, bf16[1,256,768]{2,1,0:T(8,128)(2,1)}, u32[]{:S(2)}) copy-start(bf16[1,256,768]{2,1,0:T(8,128)(2,1)} %param.15) | copy-start | bytes 1179652
  95.4 101.7 %reduce-scatter.2.cloned.1.call-start = ((), (), s32[]{:S(2)}) async-start(), calls=%async_computation.2 | async-start | bytes 3932160 | tf_op jit(solution)/shard_map/reduce_scatter | solution.py:510
  124.4 1.9 copy-start
  126.3 8.6 %copy-start.12 = (bf16[8,2,48,3072]{3,2,1,0:T(8,128)(2,1)S(1)}, bf16[8,2,48,3072]{3,2,1,0:T(8,128)(2,1)}, u32[]{:S(2)}) copy-start(bf16[8,2,48,3072]{3,2,1,0:T(8,128)(2,1)} %get-tuple-element.32) | copy-start | bytes 14155780
  134.7 2.2 slice-start
  134.9 2.1 copy-start.7
  134.9 2.2 slice-start.1
  136.4 3.8 %copy-start.13 = (f32[256,3072]{1,0:T(8,128)}, f32[256,3072]{1,0:T(8,128)S(1)}, u32[]{:S(2)}) copy-start(f32[256,3072]{1,0:T(8,128)S(1)} %convolution_add_fusion.1) | copy-start | bytes 9437188
  140.2 1.2 copy-start.8
  143.0 1.3 copy-start.6
  143.3 1.4 copy-start.3
  157.2 1.6 copy-start.1
  159.5 3.4 %copy-start.9 = (bf16[256,3072]{1,0:T(8,128)(2,1)S(1)}, bf16[256,3072]{1,0:T(8,128)(2,1)}, u32[]{:S(2)}) copy-start(bf16[256,3072]{1,0:T(8,128)(2,1)} %copy-done.8) | copy-start | bytes 4718596
  163.0 4.1 %copy-start.14 = (f32[256,3072]{1,0:T(8,128)S(1)}, f32[256,3072]{1,0:T(8,128)}, u32[]{:S(2)}) copy-start(f32[256,3072]{1,0:T(8,128)} %copy-done.13) | copy-start | bytes 9437188
  163.0 8.5 %slice-start.2 = ((s8[4718592]{0:T(1024)(128)(4,1)}), s8[4194304]{0:T(1024)(128)(4,1)S(1)}, s32[]{:S(2)}) async-start(s8[4718592]{0:T(1024)(128)(4,1)} %bitcast.150), calls=%async_computation.5 | async-start | bytes 8388608
  167.1 4.4 %slice-start.3 = ((s8[4718592]{0:T(1024)(128)(4,1)}), s8[524288]{0:T(1024)(128)(4,1)S(1)}, s32[]{:S(2)}) async-start(s8[4718592]{0:T(1024)(128)(4,1)} %bitcast.150), calls=%async_computation.6 | async-start | bytes 1048576
  171.5 25.6 %copy-start.5 = (bf16[256,2304]{1,0:T(8,128)(2,1)S(1)}, bf16[256,2304]{1,0:T(8,128)(2,1)}, u32[]{:S(2)}) copy-start(bf16[256,2304]{1,0:T(8,128)(2,1)} %constant_dynamic-update-slice_fusion.1) | copy-start | bytes 3538948
  311.0 8.4 %copy-start.10 = (bf16[2,192,768]{2,1,0:T(8,128)(2,1)S(1)}, bf16[2,192,768]{2,1,0:T(8,128)(2,1)}, u32[]{:S(2)}) copy-start(bf16[2,192,768]{2,1,0:T(8,128)(2,1)} %get-tuple-element.41) | copy-start | bytes 1769476
  311.1 9.5 %copy-start.4 = (f32[256,768]{1,0:T(8,128)S(1)}, f32[256,768]{1,0:T(8,128)}, u32[]{:S(2)}) copy-start(f32[256,768]{1,0:T(8,128)} %copy-done.3) | copy-start | bytes 2359300
Sparse Core Ops, SparseCore 0:
  95.5 28.8 all-gather.1
  159.0 38.0 reduce-scatter.1

commit v3 on v2

--- a/solution.py
+++ b/solution.py
@@ -62,7 +62,7 @@
     return picked * block_rows + row_index % block_rows
 
 
-def attend_kernel(query_place, key_place, q_ref, kv_ref, out_ref, log_ref):
+def attend_part(query_place, key_place, q_ref, kv_ref, out_ref, log_ref):
     rows, width = q_ref.shape
     head_dim = width // HEADS
     per_group = LANES // head_dim
@@ -72,8 +72,8 @@
     for group in range(width // LANES):
         span = pl.ds(group * LANES, LANES)
         q = q_ref[:, span] * (head_dim**-0.5)
-        k = kv_ref[:, span]
-        v = kv_ref[:, pl.ds(width + group * LANES, LANES)]
+        k = kv_ref[:, :, span].reshape(-1, LANES)
+        v = kv_ref[:, :, pl.ds(width + group * LANES, LANES)].reshape(-1, LANES)
         out = jnp.zeros((rows, LANES), F32)
         for part in range(per_group):
             own = lane // head_dim == part
@@ -88,8 +88,8 @@
     log_ref[...] = logs
 
 
-def attend_back_kernel(
-    query_place, key_place, q_ref, kv_ref, att_ref, grad_ref, log_ref, dq_ref, dkv_ref
+def attend_back_part(
+    groups, query_place, key_place, q_ref, kv_ref, att_ref, grad_ref, log_ref, dq_ref, dkv_ref
 ):
     rows, width = q_ref.shape
     head_dim = width // HEADS
@@ -97,12 +97,12 @@
     scale = head_dim**-0.5
     visible = key_place[...] <= query_place[...]
     lane = lax.broadcasted_iota(jnp.int32, (rows, LANES), 1)
-    for group in range(width // LANES):
+    for group in groups:
         span = pl.ds(group * LANES, LANES)
         far = pl.ds(width + group * LANES, LANES)
         q = q_ref[:, span] * scale
-        k = kv_ref[:, span]
-        v = kv_ref[:, far]
+        k = kv_ref[:, :, span].reshape(-1, LANES)
+        v = kv_ref[:, :, far].reshape(-1, LANES)
         grad = grad_ref[:, span]
         product = grad.astype(F32) * att_ref[:, span]
         dq = jnp.zeros((rows, LANES), F32)
@@ -125,35 +125,12 @@
             dq = jnp.where(own, dot(change, k) * scale, dq)
             dk = dk + dot_rows(change, own_q)
         dq_ref[:, span] = dq.astype(BF16)
-        dkv_ref[:, span] = dk.astype(BF16)
-        dkv_ref[:, far] = dv.astype(BF16)
-
-
-def attend(query_place, key_place, q, kv):
-    rows, width = q.shape
-    return pl.pallas_call(
-        attend_kernel,
-        out_shape=(
-            jax.ShapeDtypeStruct((rows, width), F32),
-            jax.ShapeDtypeStruct((rows, LANES), F32),
-        ),
-        compiler_params=pltpu.CompilerParams(vmem_limit_bytes=48 * 2**20),
-    )(query_place, key_place, q, kv)
-
-
-def attend_back(query_place, key_place, q, kv, attended, grad, logs):
-    return pl.pallas_call(
-        attend_back_kernel,
-        out_shape=(
-            jax.ShapeDtypeStruct(q.shape, BF16),
-            jax.ShapeDtypeStruct(kv.shape, BF16),
-        ),
-        compiler_params=pltpu.CompilerParams(vmem_limit_bytes=48 * 2**20),
-    )(query_place, key_place, q, kv, attended, grad, logs)
+        shape = (kv_ref.shape[0], rows, LANES)
+        dkv_ref[:, :, span] = dk.astype(BF16).reshape(shape)
+        dkv_ref[:, :, far] = dv.astype(BF16).reshape(shape)
+
 
 MESH = pl.DeviceIdType.MESH
-GATHER_ID = 0
-REDUCE_ID = 1
 
 
 def ring_order(fsdp, depth):
@@ -195,9 +172,49 @@
     pl.semaphore_wait(barrier, len(devices))
 
 
-def gather_kernel(order, count, *refs):
-    ins, outs = refs[:count], refs[count : 2 * count]
-    send, receive, pair_send, pair_receive, local = refs[2 * count :]
+def attend_hooks(lines, ctx, sibling, peers, pending, ins, outs, sems):
+    query_place, key_place, q_ref, own_ref = ins
+    kv_ref, out_ref, log_ref = outs
+    send, receive, pair_send, pair_receive = sems
+    core, line = lax.rem(ctx, 2), ctx // 2
+
+    def to_sibling(source, at, slot):
+        copy = remote(source, kv_ref.at[at], pair_send.at[slot], pair_receive.at[slot], sibling)
+        copy.start()
+        pending.append(copy)
+
+    def begin():
+        for k in range(1, lines):
+            copy = remote(
+                own_ref, kv_ref.at[ctx], send.at[k - 1], receive.at[k - 1], peers[k - 1]
+            )
+            copy.start()
+            pending.append(copy)
+        to_sibling(own_ref, ctx, 0)
+        kv_ref[ctx] = own_ref[...]
+
+    def relay():
+        for k in range(1, lines):
+            at = lax.rem(line + lines - k, lines) * 2 + core
+            target = kv_ref.at[at]
+            remote(target, target, send.at[k - 1], receive.at[k - 1], peers[k - 1]).wait_recv()
+            to_sibling(target, at, k)
+
+    def compute():
+        for k in range(lines):
+            target = kv_ref.at[lax.rem(line + lines - k, lines) * 2 + 1 - core]
+            remote(target, target, pair_send.at[k], pair_receive.at[k], sibling).wait_recv()
+        attend_part(query_place, key_place, q_ref, kv_ref, out_ref, log_ref)
+
+    return {0: begin, 1: relay, 2: compute}
+
+
+def gather_kernel(order, lines, count, extra, *refs):
+    ins, side_in = refs[:count], refs[count : count + extra[0]]
+    refs = refs[count + extra[0] :]
+    outs, side_out = refs[:count], refs[count : count + extra[1]]
+    refs = refs[count + extra[1] :]
+    send, receive, pair_send, pair_receive, local = refs[:5]
     size = len(order)
     me, ctx = lax.axis_index("fsdp"), lax.axis_index("ctx")
     core = lax.rem(ctx, 2)
@@ -205,13 +222,18 @@
     inverse = [order.index(at) for at in range(size)]
     block = ring_blocks(order, pick(inverse, me))
     following, preceding = (block[1], ctx), (block[size - 1], ctx)
-    greet([following, preceding, sibling])
+    line = ctx // 2
+    peers = [(me, lax.rem(line + k, lines) * 2 + core) for k in range(1, lines)]
+    greet([following, preceding, sibling] + (peers if side_in else []))
     started = []
     for a in range(count):
         copy = pltpu.make_async_copy(ins[a].at[core], outs[a].at[me, core], local.at[a])
         copy.start()
         started.append(copy)
     pending = []
+    hooks = {}
+    if side_in:
+        hooks = attend_hooks(lines, ctx, sibling, peers, pending, side_in, side_out, refs[5:])
     hops = [(size // 2, size - 1 - size // 2), (size - 1 - size // 2, size // 2)]
     for step in range(size // 2 + 1):
         for a in range(count):
@@ -239,6 +261,8 @@
                     )
                     copy.start()
                     pending.append(copy)
+        if step in hooks:
+            hooks[step]()
     for a in range(count):
         for shift in range(size):
             target = outs[a].at[block[shift], 1 - core]
@@ -251,32 +275,94 @@
         copy.wait()
 
 
-def gather_all(shards, order):
+def gather_all(shards, order, lines, collective_id, side=()):
     count, size = len(shards), len(order)
     dma = pltpu.SemaphoreType.DMA
+    any_space = pl.BlockSpec(memory_space=pl.ANY)
+    vmem = pl.BlockSpec(memory_space=pltpu.VMEM)
+    side_out, sems = [], []
+    if side:
+        rows, width = side[2].shape
+        side_out = [
+            jax.ShapeDtypeStruct((2 * lines,) + side[3].shape, BF16),
+            jax.ShapeDtypeStruct((rows, width), F32),
+            jax.ShapeDtypeStruct((rows, LANES), F32),
+        ]
+        sems = [dma((max(lines - 1, 1),)), dma((max(lines - 1, 1),)), dma((lines,)), dma((lines,))]
     return pl.pallas_call(
-        partial(gather_kernel, order, count),
-        out_shape=[jax.ShapeDtypeStruct((size,) + s.shape, s.dtype) for s in shards],
-        in_specs=[pl.BlockSpec(memory_space=pl.ANY)] * count,
-        out_specs=[pl.BlockSpec(memory_space=pl.ANY)] * count,
+        partial(gather_kernel, order, lines, count, (len(side), len(side_out))),
+        out_shape=[jax.ShapeDtypeStruct((size,) + s.shape, s.dtype) for s in shards] + side_out,
+        in_specs=[any_space] * count + [vmem] * len(side),
+        out_specs=[any_space] * count + [vmem] * len(side_out),
         scratch_shapes=[
             dma((count, 2, size // 2)),
             dma((count, 2, size // 2)),
             dma((count, size)),
             dma((count, size)),
             dma((count,)),
-        ],
-        compiler_params=pltpu.CompilerParams(collective_id=GATHER_ID, has_side_effects=True),
-    )(*shards)
-
-
-def reduce_kernel(order, lines, count, *refs):
-    ins, outs = refs[:count], refs[count : 2 * count]
-    pairs = refs[2 * count : 3 * count]
-    slots = refs[3 * count : 4 * count]
-    crossed = refs[4 * count : 5 * count]
-    ring_send, ring_receive, pair_send, pair_receive = refs[5 * count : 5 * count + 4]
-    line_send, line_receive, last_send, last_receive = refs[5 * count + 4 :]
+        ]
+        + sems,
+        compiler_params=pltpu.CompilerParams(
+            collective_id=collective_id, has_side_effects=True, vmem_limit_bytes=48 * 2**20
+        ),
+    )(*shards, *side)
+
+
+def attend_back_hooks(lines, ctx, sibling, peers, pending, ins, outs, scratch):
+    dq_ref, own_ref = outs
+    dkv_ref, pair_ref, sum_ref, line_ref, pair_send, pair_receive, send, receive = scratch
+    core, line = lax.rem(ctx, 2), ctx // 2
+    groups = dq_ref.shape[1] // LANES
+
+    def compute(third):
+        span = range(third * groups // 3, (third + 1) * groups // 3)
+        attend_back_part(span, *ins, dq_ref, dkv_ref)
+
+    def begin():
+        compute(2)
+        for k in range(lines):
+            at = lax.rem(line + k, lines)
+            copy = remote(
+                dkv_ref.at[2 * at + 1 - core], pair_ref.at[at],
+                pair_send.at[k], pair_receive.at[k], sibling,
+            )
+            copy.start()
+            pending.append(copy)
+
+    def relay():
+        for k in list(range(1, lines)) + [0]:
+            at = lax.rem(line + k, lines)
+            target = pair_ref.at[at]
+            remote(target, target, pair_send.at[k], pair_receive.at[k], sibling).wait_recv()
+            value = dkv_ref[2 * at + core].astype(F32) + pair_ref[at].astype(F32)
+            sum_ref[k] = value.astype(BF16)
+            if k:
+                copy = remote(
+                    sum_ref.at[k], line_ref.at[k - 1], send.at[k - 1], receive.at[k - 1],
+                    peers[k - 1],
+                )
+                copy.start()
+                pending.append(copy)
+
+    def finish():
+        value = sum_ref[0].astype(F32)
+        for k in range(1, lines):
+            target = line_ref.at[k - 1]
+            remote(target, target, send.at[k - 1], receive.at[k - 1], peers[k - 1]).wait_recv()
+            value = value + line_ref[k - 1].astype(F32)
+        own_ref[...] = value.astype(BF16)
+
+    return {0: partial(compute, 0), 1: partial(compute, 1), 2: begin, 4: relay, 7: finish}
+
+
+def reduce_kernel(order, lines, count, extra, *refs):
+    ins, side_in = refs[:count], refs[count : count + extra[0]]
+    refs = refs[count + extra[0] :]
+    outs, side_out = refs[:count], refs[count : count + extra[1]]
+    refs = refs[count + extra[1] :]
+    pairs, slots, crossed = refs[:count], refs[count : 2 * count], refs[2 * count : 3 * count]
+    ring_send, ring_receive, pair_send, pair_receive = refs[3 * count : 3 * count + 4]
+    line_send, line_receive, last_send, last_receive = refs[3 * count + 4 : 3 * count + 8]
     size = len(order)
     me, ctx = lax.axis_index("fsdp"), lax.axis_index("ctx")
     core = lax.rem(ctx, 2)
@@ -288,6 +374,12 @@
     peers = [(me, lax.rem(line + k, lines) * 2 + core) for k in range(1, lines)]
     greet(ways + [sibling] + peers)
     pending = []
+    hooks = {}
+    if side_in:
+        side_scratch = refs[3 * count + 8 :]
+        hooks = attend_back_hooks(
+            lines, ctx, sibling, peers, pending, side_in, side_out, side_scratch
+        )
 
     def shift_of(way, step):
         return (size - 1 - step) % size if way == 0 else (1 + step) % size
@@ -343,6 +435,8 @@
                     pending.append(copy)
                 else:
                     crossed[a][line, :, span] = value.astype(BF16)
+        if step in hooks and step != 7:
+            hooks[step]()
     for a in range(count):
         for k in range(1, lines):
             copy = remote(
@@ -351,6 +445,8 @@
             )
             copy.start()
             pending.append(copy)
+    if side_in:
+        hooks[7]()
     for a in range(count):
         for k in range(1, lines):
             target = crossed[a].at[lax.rem(line + lines - k, lines)]
@@ -373,7 +469,7 @@
         copy.wait_send()
 
 
-def reduce_all(grads, order, lines):
+def reduce_all(grads, order, lines, collective_id, side=()):
     count, size = len(grads), len(order)
     dma = pltpu.SemaphoreType.DMA
     vmem = pl.BlockSpec(memory_space=pltpu.VMEM)
@@ -384,16 +480,28 @@
     scratch += [dma((count, size)), dma((count, size))]
     scratch += [dma((count, max(lines - 1, 1))), dma((count, max(lines - 1, 1)))]
     scratch += [dma((count,)), dma((count,))]
+    side_out = []
+    if side:
+        rows, both = side[3].shape[1:]
+        side_out = [
+            jax.ShapeDtypeStruct(side[2].shape, BF16),
+            jax.ShapeDtypeStruct((rows, both), BF16),
+        ]
+        scratch += [pltpu.VMEM((2 * lines, rows, both), BF16)]
+        scratch += [pltpu.VMEM((lines, rows, both), BF16)] * 2
+        scratch += [pltpu.VMEM((max(lines - 1, 1), rows, both), BF16)]
+        scratch += [dma((lines,)), dma((lines,))]
+        scratch += [dma((max(lines - 1, 1),)), dma((max(lines - 1, 1),))]
     return pl.pallas_call(
-        partial(reduce_kernel, order, lines, count),
-        out_shape=[jax.ShapeDtypeStruct(g.shape[1:], BF16) for g in grads],
-        in_specs=[vmem] * count,
-        out_specs=[vmem] * count,
+        partial(reduce_kernel, order, lines, count, (len(side), len(side_out))),
+        out_shape=[jax.ShapeDtypeStruct(g.shape[1:], BF16) for g in grads] + side_out,
+        in_specs=[vmem] * (count + len(side)),
+        out_specs=[vmem] * (count + len(side_out)),
         scratch_shapes=scratch,
         compiler_params=pltpu.CompilerParams(
-            collective_id=REDUCE_ID, has_side_effects=True, vmem_limit_bytes=56 * 2**20
+            collective_id=collective_id, has_side_effects=True, vmem_limit_bytes=56 * 2**20
         ),
-    )(*grads)
+    )(*grads, *side)
 
 
 def round_up(value, unit):
@@ -462,13 +570,8 @@
     )
     small_rows = small.shape[0]
     small = pad_to(small, (2 * sixteen, round_up(shard, LANES))).reshape(2, sixteen, -1)
-    qkv_full, fc_full, out_full, proj_full, small = gather_all(
-        [two(w_qkv), two(w_fc), two(w_out), two(w_proj), small], order
-    )
+    qkv_full, small = gather_all([two(w_qkv), small], order, lines, 0)
     qkv_full = full(qkv_full, w_qkv)
-    fc_full = full(fc_full, w_fc)
-    out_full = full(out_full, w_out)
-    proj_full = full(proj_full, w_proj)
     small = small.reshape(spread, 2 * sixteen, -1)[:, :small_rows, :shard].astype(F32)
     vectors = jnp.moveaxis(small[:, :8], 0, 1).reshape(8, width)
     gain_one, shift_one, q_bias, v_bias, out_shift, gain_two, shift_two, proj_shift = vectors
@@ -480,11 +583,19 @@
     qkv_shift = jnp.concatenate([q_bias, jnp.zeros_like(q_bias), v_bias])
     qkv = (dot(normed_one, qkv_full) + qkv_shift).astype(BF16)
     q = qkv[:, :width]
-    kv = lax.all_gather(qkv[:, width:], "ctx", axis=0, tiled=True)
-    block_rows = kv.shape[0] // block_order.shape[0]
+    block_rows = rows * positions // block_order.shape[0]
     query_place = block_places(block_order, place * rows, rows, block_rows)[:, None]
-    key_place = block_places(block_order, jnp.int32(0), kv.shape[0], block_rows)[None]
-    attended, logs = attend(query_place, key_place, q, kv)
+    key_place = block_places(block_order, jnp.int32(0), rows * positions, block_rows)[None]
+    fc_full, proj_full, out_full, kv, attended, logs = gather_all(
+        [two(w_fc), two(w_proj), two(w_out)],
+        order,
+        lines,
+        1,
+        (query_place, key_place, q, qkv[:, width:]),
+    )
+    fc_full = full(fc_full, w_fc)
+    proj_full = full(proj_full, w_proj)
+    out_full = full(out_full, w_out)
     attended_low = attended.astype(BF16)
     middle = tokens + dot(attended_low, out_full) + out_shift
     unit_two, inverse_two = normalise(middle)
@@ -506,8 +617,13 @@
     grad_branch = grad_middle.astype(BF16)
     out_grad = dot_rows(attended_low, grad_branch)
     grad_attended = dot_lanes(grad_branch, out_full).astype(BF16)
-    dq, dkv = attend_back(query_place, key_place, q, kv, attended, grad_attended, logs)
-    dkv = lax.psum_scatter(dkv, "ctx", scatter_dimension=0, tiled=True)
+    fc_grad, proj_grad, out_grad, dq, dkv = reduce_all(
+        [spread_out(fc_grad), spread_out(proj_grad), spread_out(out_grad)],
+        order,
+        lines,
+        2,
+        (query_place, key_place, q, kv, attended, grad_attended, logs),
+    )
     grad_qkv = jnp.concatenate([dq, dkv], axis=1)
     qkv_grad = dot_rows(normed_one, grad_qkv)
     grad_normed_one = dot_lanes(grad_qkv, qkv_full)
@@ -536,16 +652,8 @@
     small_grad = pad_to(
         small_grad, (spread, 2 * sixteen, round_up(shard, 2 * LANES))
     ).reshape(spread, 2, sixteen, -1)
-    qkv_grad, fc_grad, out_grad, proj_grad, small_grad = reduce_all(
-        [
-            spread_out(qkv_grad),
-            spread_out(fc_grad),
-            spread_out(out_grad),
-            spread_out(proj_grad),
-            small_grad.astype(BF16),
-        ],
-        order,
-        lines,
+    qkv_grad, small_grad = reduce_all(
+        [spread_out(qkv_grad), small_grad.astype(BF16)], order, lines, 3
     )
     small_grad = small_grad.reshape(2 * sixteen, -1)[:small_rows, :shard].astype(F32)
 

time: 332 us -> 270 us (0.81)
  waiting for transfers between devices: 50.9 us -> 0 us
  between operations: 14.6 us -> 1.31 us
  Pallas kernels: 202 us -> 210 us
  local copies, waits for them, and re-layouts: 15.6 us -> 11.6 us
    all_gather x1 -> x0, waiting for transfers between devices: 28 us -> none  [shards(): kv = lax.all_gather(qkv[:, width:], 'ctx', axis=0, tiled=True)]
    reduce_scatter x1 -> x0, waiting for transfers between devices: 22.9 us -> none  [shards(): dkv = lax.psum_scatter(dkv, 'ctx', scatter_dimension=0, tiled=True)]
    pallas_call x4, Pallas kernels: 202 us -> 210 us  [the longest x2 122 us: reduce_all(): pl.pallas_call(partial(reduce_kernel, order, lines, count, (len(side), le...]
    unnamed x47 -> x67, local copies, waits for them, and re-layouts: 7.19 us -> 4.07 us
  transfers between devices with their start and end apart: 2 -> 0, of which waited for: 2 -> 0; matrix products, arithmetic and copies ran while one was open for 5% -> 0% of each run, Pallas kernels for 0% -> 0%
where the time goes in v3:
time: 270 us; the launch traced here: 267 us
  Pallas kernels  210 us (78%)
  matrix products  31.8 us (12%)
  other arithmetic  12.2 us (5%)
  local copies, waits for them, and re-layouts  11.6 us (4%)
    pallas_call x2, Pallas kernels, reduce_all(): pl.pallas_call(partial(reduce_kernel, order, lines, count, (len(side), le...  122 us
    pallas_call x2, Pallas kernels, gather_all(): pl.pallas_call(partial(gather_kernel, order, lines, count, (len(side), le...  87.7 us
    dot_general x4, matrix products, dot_rows(): return lax.dot_general(left, right, ROW_DOT, preferred_element_type=F32)  12.7 us
    dot_general x4, matrix products, dot(): return jnp.dot(left, right, preferred_element_type=F32)  10.6 us
    dot_general x4, matrix products, dot_lanes(): return lax.dot_general(left, right, LANE_DOT, preferred_element_type=F32)  8.49 us

profile of v3, /device:TPU:0, one launch (start us, length us, event | category | flops | bytes accessed | tf_op | source)
XLA Modules:
  0.0 267.0 jit_solution(1667195553538116257)
XLA Ops:
  0.6 0.8 reshape.344
  1.4 0.8 concatenate.15
  2.2 1.0 copy-done.5
  3.2 30.1 %shard_map.254 = (bf16[8,2,48,2304]{3,2,1,0:T(8,128)(2,1)S(1)}, bf16[8,2,16,128]{3,2,1,0:T(8,128)(2,1)S(1)}) custom-call(bf16[2,48,2304]{2,1,0:T(8,128)(2,1)S(1)} %bitcast.128, bf16[2,16,128]{2,1,0:T(8,128)(2,1)S(1)} %bitcast.130), custom_call_target="tpu_custom_call" | custom-call | tf_op jit(solution)/shard_map/pallas_call | solution.py:292
  33.4 1.8 copy-done.9
  35.1 0.1 slice_reduce_fusion.2
  35.3 0.7 select_reduce_fusion.1
  36.1 0.1 copy.34
  36.3 0.8 select_reduce_fusion
  37.5 1.1 convert_reduce_fusion
  38.6 1.2 fusion.28
  39.9 3.4 %fusion.2 = bf16[256,2304]{1,0:T(8,128)(2,1)S(1)} fusion(bf16[768,2304]{1,0:T(8,128)(2,1)} %bitcast.132, f32[2304]{0:T(1024)S(1)} %pad_maximum_fusion.1, bf16[1,256,768]{2,1,0:T(8,128)(2,1)} %param.15, f32[768]{0:T(1024)S(1)} %add.193, f32[768]{0:T(1024)S(1)} %mul.192, f32[256]{0:T(256)S(1)} %add_rsqrt_fusion.1, f32[256]{0:T(256)S(1)} %broadcast_multiply_fusion.6), kind=kOutput, calls=%fused_computation.10 | convolution fusion | flops 908328960 | bytes 5129216 | tf_op jit(solution)/shard_map/dot_general | solution.py:21
  43.5 57.6 %shard_map.255 = (bf16[8,2,48,3072]{3,2,1,0:T(8,128)(2,1)}, bf16[8,2,192,768]{3,2,1,0:T(8,128)(2,1)}, bf16[8,2,48,768]{3,2,1,0:T(8,128)(2,1)S(1)}, bf16[4,256,15...) custom-call(bf16[2,48,3072]{2,1,0:T(8,128)(2,1)S(1)} %bitcast.126, ...), custom_call_target="tpu_custom_call" | custom-call | tf_op jit(solution)/shard_map/pallas_call | solution.py:292
  101.2 0.6 fusion.61
  101.8 0.7 add.212
  102.7 0.2 multiply_reduce_fusion.2
  102.9 4.0 %convolution_add_fusion.1 = f32[256,3072]{1,0:T(8,128)S(1)} fusion(bf16[768,3072]{1,0:T(8,128)(2,1)} %bitcast.149, f32[3072]{0:T(1024)S(1)} %add.206, f32[256,768]{1,0:T(8,128)S(1)} %get-tuple-element.71, f32[768]{0:T(1024)S(1)} %add.203, f32[768]{0:T(1024)S(1)} %mul.198, f32[256]{0:T(256)S(1)} %add_rsqrt_fusion, f32[256]{0:T(256)S(1)} %broadcast_multiply_fusion.5), kind=kOutput, calls=%fused_computation.8 | convolution fusion | flops 1209729024 | bytes 8671232 | tf_op jit(solution)/shard_map/dot_general | solution.py:21
  107.0 2.7 %fusion.12 = bf16[1,256,768]{2,1,0:T(8,128)(2,1)} fusion(f32[256,768]{1,0:T(8,128)S(1)} %get-tuple-element.71, bf16[3072,768]{1,0:T(8,128)(2,1)S(1)} %bitcast.155, f32[768]{0:T(1024)S(1)} %copy-done.22, f32[256,3072]{1,0:T(8,128)S(1)} %convolution_add_fusion.1), kind=kOutput, calls=%fused_computation.25 | convolution fusion | flops 1215627264 | bytes 9047040 | tf_op jit(solution)/shard_map/dot_general | solution.py:21
  109.7 3.8 %fusion.62 = (bf16[3072]{0:T(1024)(128)(2,1)}, bf16[256,3072]{1,0:T(8,128)(2,1)S(1)}) fusion(f32[256,3072]{1,0:T(8,128)S(1)} %convolution_add_fusion.1, bf16[3072,768]{1,0:T(8,128)(2,1)S(1)} %bitcast.156, bf16[1,256,768]{2,1,0:T(8,128)(2,1)S(1)} %copy-done.12), kind=kOutput, calls=%fused_computation.144 | convolution fusion | flops 1223685120 | bytes 9836544 | tf_op jit(solution)/shard_map/dot_general | solution.py:29
  113.5 2.2 multiply_reduce_fusion
  115.6 0.9 convert_reduce_fusion.1
  116.6 3.7 %convolution_convert_fusion.2 = bf16[768,3072]{1,0:T(8,128)(2,1)} fusion(bf16[256,3072]{1,0:T(8,128)(2,1)S(1)} %get-tuple-element.75, f32[256,768]{1,0:T(8,128)S(1)} %get-tuple-element.71, f32[768]{0:T(1024)S(1)} %add.203, f32[768]{0:T(1024)S(1)} %mul.198, f32[256]{0:T(256)S(1)} %add_rsqrt_fusion, f32[256]{0:T(256)S(1)} %broadcast_multiply_fusion.5), kind=kOutput, calls=%fused_computation.2 | convolution fusion | flops 1211301888 | bytes 7086080 | tf_op jit(solution)/shard_map/dot_general | solution.py:25
  120.3 4.4 %convolution_convert_fusion.1 = bf16[3072,768]{1,0:T(8,128)(2,1)} fusion(bf16[1,256,768]{2,1,0:T(8,128)(2,1)S(1)} %copy-done.12, f32[256,3072]{1,0:T(8,128)S(1)} %convolution_add_fusion.1), kind=kOutput, calls=%fused_computation.1 | convolution fusion | flops 1217396736 | bytes 8257536 | tf_op jit(solution)/shard_map/dot_general | solution.py:25
  124.7 1.5 convolution_convert_fusion.3
  126.2 1.3 convolution_convert_fusion.4.refs_8_
  127.5 80.1 %shard_map.256 = (bf16[2,48,3072]{2,1,0:T(8,128)(2,1)}, bf16[2,192,768]{2,1,0:T(8,128)(2,1)}, bf16[2,48,768]{2,1,0:T(8,128)(2,1)}, bf16[256,768]{1,0:T(8,128)(2,1)}, bf16[256,1536]{1,0:T(8,128)(2,1)}) custom-call(bf16[8,2,48,3072]{3,2,1,0:T(8,128)(2,1)} %bitcast.134, bf16[8,2,192,768]{3,2,1,0:T(8,128)(2,1)} %bitcast.137, bf16[8,2,48,768]{3,2,1,0:T(8,128)(2,1)} %bitcast.136, ...), custom_call_target="tpu_custom_call" | custom-call | tf_op jit(solution)/shard_map/pallas_call | solution.py:495
  207.5 1.0 constant_dynamic-update-slice_fusion.1
  208.6 1.2 constant_dynamic-update-slice_fusion
  209.8 1.3 fusion.27
  211.1 1.1 fusion.36
  212.2 3.0 %convolution_convert_fusion = bf16[768,2304]{1,0:T(8,128)(2,1)} fusion(bf16[256,2304]{1,0:T(8,128)(2,1)S(1)} %constant_dynamic-update-slice_fusion, bf16[1,256,768]{2,1,0:T(8,128)(2,1)S(1)} %copy-done.11, f32[768]{0:T(1024)S(1)} %add.193, f32[768]{0:T(1024)S(1)} %mul.192, f32[256]{0:T(256)S(1)} %copy-done.19, f32[256]{0:T(256)S(1)} %copy-done.17), kind=kOutput, calls=%fused_computation | convolution fusion | flops 908918784 | bytes 5120000 | tf_op jit(solution)/shard_map/dot_general | solution.py:25
  215.2 0.1 reshape.355
  215.3 0.1 stack.27
  215.4 0.1 stack.28
  215.5 0.2 reduce.1
  215.7 0.1 stack.29
  216.2 0.1 reduce.3
  216.3 0.1 stack.34
  216.4 0.7 pad.10.clone
  217.1 42.2 %shard_map.257 = (bf16[2,48,2304]{2,1,0:T(8,128)(2,1)}, bf16[2,16,256]{2,1,0:T(8,128)(2,1)}) custom-call(bf16[8,2,48,2304]{3,2,1,0:T(8,128)(2,1)} %bitcast.135, bf16[8,2,16,256]{3,2,1,0:T(8,128)(2,1)} %bitcast.138), custom_call_target="tpu_custom_call" | custom-call | tf_op jit(solution)/shard_map/pallas_call | solution.py:495
  259.3 0.7 slice_convert_fusion.1
  260.0 0.5 slice_bitcast_fusion.1
  260.5 2.0 bitcast_convert_fusion.2
  262.5 0.6 slice.96
  263.1 0.7 bitcast_convert_fusion.3
  263.8 1.2 bitcast_convert_fusion.1
  265.0 0.7 reshape.357
  265.6 1.1 bitcast_convert_fusion
  (104 shorter events, 1.5 us)
Async XLA Ops:
  2.2 1.0 copy-start.5
  33.4 1.8 copy-start.9
  36.3 7.1 %copy-start.2 = (s32[256,1]{1,0:T(8,128)}, s32[256,1]{1,0:T(8,128)S(1)}, u32[]{:S(2)}) copy-start(s32[256,1]{1,0:T(8,128)S(1)} %fusion.50.refs_3_) | copy-start | bytes 3076
  37.1 6.3 %copy-start.8 = (s32[1,1024]{1,0:T(1,128)}, s32[1,1024]{1,0:T(1,128)S(1)}, u32[]{:S(2)}) copy-start(s32[1,1024]{1,0:T(1,128)S(1)} %fusion.54.refs_4_) | copy-start | bytes 12292
  38.6 4.7 %copy-start.16 = (f32[256]{0:T(256)}, f32[256]{0:T(256)S(1)}, u32[]{:S(2)}) copy-start(f32[256]{0:T(256)S(1)} %broadcast_multiply_fusion.6) | copy-start | bytes 3076
  39.9 3.5 %copy-start.18 = (f32[256]{0:T(256)}, f32[256]{0:T(256)S(1)}, u32[]{:S(2)}) copy-start(f32[256]{0:T(256)S(1)} %add_rsqrt_fusion.1) | copy-start | bytes 3076
  39.9 3.6 %copy-start.3 = (bf16[96,3072]{1,0:T(8,128)(2,1)S(1)}, bf16[96,3072]{1,0:T(8,128)(2,1)}, u32[]{:S(2)}) copy-start(bf16[96,3072]{1,0:T(8,128)(2,1)} %param.26) | copy-start | bytes 1769476
  39.9 3.6 %copy-start.4 = (bf16[384,768]{1,0:T(8,128)(2,1)S(1)}, bf16[384,768]{1,0:T(8,128)(2,1)}, u32[]{:S(2)}) copy-start(bf16[384,768]{1,0:T(8,128)(2,1)} %param.28) | copy-start | bytes 1769476
  39.9 3.6 %copy-start.6 = (bf16[96,768]{1,0:T(8,128)(2,1)S(1)}, bf16[96,768]{1,0:T(8,128)(2,1)}, u32[]{:S(2)}) copy-start(bf16[96,768]{1,0:T(8,128)(2,1)} %param.22) | copy-start | bytes 442372
  43.3 57.8 %copy-start.11 = (bf16[1,256,768]{2,1,0:T(8,128)(2,1)S(1)}, bf16[1,256,768]{2,1,0:T(8,128)(2,1)}, u32[]{:S(2)}) copy-start(bf16[1,256,768]{2,1,0:T(8,128)(2,1)} %param.15) | copy-start | bytes 1179652
  43.4 58.4 %copy-start.1 = (bf16[256,768]{1,0:T(8,128)(2,1)}, bf16[256,768]{1,0:T(8,128)(2,1)S(1)}, u32[]{:S(2)}) copy-start(bf16[256,768]{1,0:T(8,128)(2,1)S(1)} %slice.88.refs_5_) | copy-start | bytes 1179652
  101.1 0.7 copy-start.7
  101.1 23.5 %copy-start = (f32[256,768]{1,0:T(8,128)}, f32[256,768]{1,0:T(8,128)S(1)}, u32[]{:S(2)}) copy-start(f32[256,768]{1,0:T(8,128)S(1)} %get-tuple-element.31.refs_7_) | copy-start | bytes 2359300
  102.7 4.2 %slice-start.2 = ((s8[4718592]{0:T(1024)(128)(4,1)}), s8[4194304]{0:T(1024)(128)(4,1)S(1)}, s32[]{:S(2)}) async-start(s8[4718592]{0:T(1024)(128)(4,1)} %bitcast.153), calls=%async_computation.2 | async-start | bytes 8388608
  102.9 4.0 %copy-start.22 = (f32[768]{0:T(1024)S(1)}, f32[768]{0:T(1024)}, u32[]{:S(2)}) copy-start(f32[768]{0:T(1024)} %add.212) | copy-start | bytes 9220
  102.9 4.0 %slice-start.3 = ((s8[4718592]{0:T(1024)(128)(4,1)}), s8[524288]{0:T(1024)(128)(4,1)S(1)}, s32[]{:S(2)}) async-start(s8[4718592]{0:T(1024)(128)(4,1)} %bitcast.153), calls=%async_computation.3 | async-start | bytes 1048576
  106.9 2.7 %copy-start.12 = (bf16[1,256,768]{2,1,0:T(8,128)(2,1)S(1)}, bf16[1,256,768]{2,1,0:T(8,128)(2,1)}, u32[]{:S(2)}) copy-start(bf16[1,256,768]{2,1,0:T(8,128)(2,1)} %param.16) | copy-start | bytes 1179652
  107.0 6.5 %slice-start = ((s8[4718592]{0:T(1024)(128)(4,1)}), s8[4194304]{0:T(1024)(128)(4,1)S(1)}, s32[]{:S(2)}) async-start(s8[4718592]{0:T(1024)(128)(4,1)} %bitcast.150), calls=%async_computation | async-start | bytes 8388608
  109.7 3.8 %slice-start.1 = ((s8[4718592]{0:T(1024)(128)(4,1)}), s8[524288]{0:T(1024)(128)(4,1)S(1)}, s32[]{:S(2)}) async-start(s8[4718592]{0:T(1024)(128)(4,1)} %bitcast.150), calls=%async_computation.1 | async-start | bytes 1048576
  127.5 82.3 %copy-start.10 = (bf16[8,2,48,2304]{3,2,1,0:T(8,128)(2,1)S(1)}, bf16[8,2,48,2304]{3,2,1,0:T(8,128)(2,1)}, u32[]{:S(2)}) copy-start(bf16[8,2,48,2304]{3,2,1,0:T(8,128)(2,1)} %copy-done.9) | copy-start | bytes 10616836
  127.5 82.3 %copy-start.17 = (f32[256]{0:T(256)S(1)}, f32[256]{0:T(256)}, u32[]{:S(2)}) copy-start(f32[256]{0:T(256)} %copy-done.16) | copy-start | bytes 3076
  127.5 82.3 %copy-start.19 = (f32[256]{0:T(256)S(1)}, f32[256]{0:T(256)}, u32[]{:S(2)}) copy-start(f32[256]{0:T(256)} %copy-done.18) | copy-start | bytes 3076
  212.2 3.1 %copy-start.21 = (bf16[3072]{0:T(1024)(128)(2,1)S(1)}, bf16[3072]{0:T(1024)(128)(2,1)}, u32[]{:S(2)}) copy-start(bf16[3072]{0:T(1024)(128)(2,1)} %get-tuple-element.74) | copy-start | bytes 18436
  212.2 3.8 %copy-start.20 = (bf16[768]{0:T(1024)(128)(2,1)S(1)}, bf16[768]{0:T(1024)(128)(2,1)}, u32[]{:S(2)}) copy-start(bf16[768]{0:T(1024)(128)(2,1)} %get-tuple-element.60) | copy-start | bytes 4612
  212.2 3.9 %copy-start.24 = (bf16[768]{0:T(1024)(128)(2,1)S(1)}, bf16[768]{0:T(1024)(128)(2,1)}, u32[]{:S(2)}) copy-start(bf16[768]{0:T(1024)(128)(2,1)} %get-tuple-element.44) | copy-start | bytes 4612
  212.2 4.0 %copy-start.23 = (bf16[768]{0:T(1024)(128)(2,1)S(1)}, bf16[768]{0:T(1024)(128)(2,1)}, u32[]{:S(2)}) copy-start(bf16[768]{0:T(1024)(128)(2,1)} %get-tuple-element.50) | copy-start | bytes 4612
  215.7 47.4 %copy-start.15 = (bf16[2,48,768]{2,1,0:T(8,128)(2,1)S(1)}, bf16[2,48,768]{2,1,0:T(8,128)(2,1)}, u32[]{:S(2)}) copy-start(bf16[2,48,768]{2,1,0:T(8,128)(2,1)} %get-tuple-element.41) | copy-start | bytes 442372
  215.7 48.1 %copy-start.14 = (bf16[2,48,3072]{2,1,0:T(8,128)(2,1)S(1)}, bf16[2,48,3072]{2,1,0:T(8,128)(2,1)}, u32[]{:S(2)}) copy-start(bf16[2,48,3072]{2,1,0:T(8,128)(2,1)} %get-tuple-element.42) | copy-start | bytes 1769476
  217.1 48.5 %copy-start.13 = (bf16[2,192,768]{2,1,0:T(8,128)(2,1)S(1)}, bf16[2,192,768]{2,1,0:T(8,128)(2,1)}, u32[]{:S(2)}) copy-start(bf16[2,192,768]{2,1,0:T(8,128)(2,1)} %get-tuple-element.43) | copy-start | bytes 1769476

commit v4 on v3

--- a/solution.py
+++ b/solution.py
@@ -355,14 +355,20 @@
     return {0: partial(compute, 0), 1: partial(compute, 1), 2: begin, 4: relay, 7: finish}
 
 
-def reduce_kernel(order, lines, count, extra, *refs):
+def reduce_kernel(order, lines, count, carried, extra, *refs):
+    carry, refs = refs[:carried], refs[carried:]
     ins, side_in = refs[:count], refs[count : count + extra[0]]
     refs = refs[count + extra[0] :]
-    outs, side_out = refs[:count], refs[count : count + extra[1]]
-    refs = refs[count + extra[1] :]
-    pairs, slots, crossed = refs[:count], refs[count : 2 * count], refs[2 * count : 3 * count]
-    ring_send, ring_receive, pair_send, pair_receive = refs[3 * count : 3 * count + 4]
-    line_send, line_receive, last_send, last_receive = refs[3 * count + 4 : 3 * count + 8]
+    final = not side_in
+    made = count + carried
+    outs, side_out = refs[:made], refs[made : made + extra[1]]
+    refs = refs[made + extra[1] :]
+    pairs, slots, refs = refs[:count], refs[count : 2 * count], refs[2 * count :]
+    ring_send, ring_receive, pair_send, pair_receive = refs[:4]
+    refs = refs[4:]
+    if final:
+        line_send, line_receive, last_send, last_receive = refs[:4]
+        crossed = refs[4:]
     size = len(order)
     me, ctx = lax.axis_index("fsdp"), lax.axis_index("ctx")
     core = lax.rem(ctx, 2)
@@ -376,10 +382,32 @@
     pending = []
     hooks = {}
     if side_in:
-        side_scratch = refs[3 * count + 8 :]
-        hooks = attend_back_hooks(
-            lines, ctx, sibling, peers, pending, side_in, side_out, side_scratch
+        hooks = attend_back_hooks(lines, ctx, sibling, peers, pending, side_in, side_out, refs)
+
+    def send_lines(a):
+        for k in range(1, lines):
+            copy = remote(
+                crossed[a].at[line], crossed[a].at[line], line_send.at[a, k - 1],
+                line_receive.at[a, k - 1], peers[k - 1],
+            )
+            copy.start()
+            pending.append(copy)
+
+    def sum_lines(a):
+        for k in range(1, lines):
+            target = crossed[a].at[lax.rem(line + lines - k, lines)]
+            remote(
+                target, target, line_send.at[a, k - 1], line_receive.at[a, k - 1], peers[k - 1]
+            ).wait_recv()
+        value = crossed[a][0].astype(F32)
+        for k in range(1, lines):
+            value = value + crossed[a][k].astype(F32)
+        outs[a][core] = value.astype(BF16)
+        copy = remote(
+            outs[a].at[core], outs[a].at[core], last_send.at[a], last_receive.at[a], sibling
         )
+        copy.start()
+        pending.append(copy)
 
     def shift_of(way, step):
         return (size - 1 - step) % size if way == 0 else (1 + step) % size
@@ -397,6 +425,9 @@
                     )
                     copy.start()
                     pending.append(copy)
+    for a in range(count, made):
+        crossed[a][line] = carry[a - count][...]
+        send_lines(a)
     waited = []
 
     def arrive(shift):
@@ -433,53 +464,44 @@
                     )
                     copy.start()
                     pending.append(copy)
+                elif final:
+                    crossed[a][line, :, span] = value.astype(BF16)
                 else:
-                    crossed[a][line, :, span] = value.astype(BF16)
+                    outs[a][:, span] = value.astype(BF16)
         if step in hooks and step != 7:
             hooks[step]()
-    for a in range(count):
-        for k in range(1, lines):
-            copy = remote(
-                crossed[a].at[line], crossed[a].at[line], line_send.at[a, k - 1],
-                line_receive.at[a, k - 1], peers[k - 1],
-            )
-            copy.start()
-            pending.append(copy)
+        if step == size - 2:
+            for a in range(count, made):
+                sum_lines(a)
     if side_in:
         hooks[7]()
-    for a in range(count):
-        for k in range(1, lines):
-            target = crossed[a].at[lax.rem(line + lines - k, lines)]
-            remote(
-                target, target, line_send.at[a, k - 1], line_receive.at[a, k - 1], peers[k - 1]
-            ).wait_recv()
-        value = crossed[a][0].astype(F32)
-        for k in range(1, lines):
-            value = value + crossed[a][k].astype(F32)
-        outs[a][core] = value.astype(BF16)
-        copy = remote(
-            outs[a].at[core], outs[a].at[core], last_send.at[a], last_receive.at[a], sibling
-        )
-        copy.start()
-        pending.append(copy)
-    for a in range(count):
-        target = outs[a].at[1 - core]
-        remote(target, target, last_send.at[a], last_receive.at[a], sibling).wait_recv()
+    if final:
+        for a in range(count):
+            send_lines(a)
+        for a in range(count):
+            sum_lines(a)
+        for a in range(made):
+            target = outs[a].at[1 - core]
+            remote(target, target, last_send.at[a], last_receive.at[a], sibling).wait_recv()
     for copy in pending:
         copy.wait_send()
 
 
-def reduce_all(grads, order, lines, collective_id, side=()):
+def reduce_all(grads, order, lines, collective_id, side=(), carry=()):
     count, size = len(grads), len(order)
     dma = pltpu.SemaphoreType.DMA
     vmem = pl.BlockSpec(memory_space=pltpu.VMEM)
     scratch = [pltpu.VMEM((size,) + g.shape[2:], BF16) for g in grads]
     scratch += [pltpu.VMEM((2, size, g.shape[2], g.shape[3] // 2), BF16) for g in grads]
-    scratch += [pltpu.VMEM((lines,) + g.shape[2:], BF16) for g in grads]
     scratch += [dma((count, 2, size - 1)), dma((count, 2, size - 1))]
     scratch += [dma((count, size)), dma((count, size))]
-    scratch += [dma((count, max(lines - 1, 1))), dma((count, max(lines - 1, 1)))]
-    scratch += [dma((count,)), dma((count,))]
+    made = count + len(carry)
+    parts = [g.shape[2:] for g in grads] + [c.shape for c in carry]
+    if not side:
+        scratch += [dma((made, max(lines - 1, 1))), dma((made, max(lines - 1, 1)))]
+        scratch += [dma((made,)), dma((made,))]
+        scratch += [pltpu.VMEM((lines,) + part, BF16) for part in parts]
+        parts = [(2,) + part for part in parts]
     side_out = []
     if side:
         rows, both = side[3].shape[1:]
@@ -493,15 +515,15 @@
         scratch += [dma((lines,)), dma((lines,))]
         scratch += [dma((max(lines - 1, 1),)), dma((max(lines - 1, 1),))]
     return pl.pallas_call(
-        partial(reduce_kernel, order, lines, count, (len(side), len(side_out))),
-        out_shape=[jax.ShapeDtypeStruct(g.shape[1:], BF16) for g in grads] + side_out,
-        in_specs=[vmem] * (count + len(side)),
-        out_specs=[vmem] * (count + len(side_out)),
+        partial(reduce_kernel, order, lines, count, len(carry), (len(side), len(side_out))),
+        out_shape=[jax.ShapeDtypeStruct(part, BF16) for part in parts] + side_out,
+        in_specs=[vmem] * (made + len(side)),
+        out_specs=[vmem] * (made + len(side_out)),
         scratch_shapes=scratch,
         compiler_params=pltpu.CompilerParams(
             collective_id=collective_id, has_side_effects=True, vmem_limit_bytes=56 * 2**20
         ),
-    )(*grads, *side)
+    )(*carry, *grads, *side)
 
 
 def round_up(value, unit):
@@ -652,8 +674,12 @@
     small_grad = pad_to(
         small_grad, (spread, 2 * sixteen, round_up(shard, 2 * LANES))
     ).reshape(spread, 2, sixteen, -1)
-    qkv_grad, small_grad = reduce_all(
-        [spread_out(qkv_grad), small_grad.astype(BF16)], order, lines, 3
+    qkv_grad, small_grad, fc_grad, proj_grad, out_grad = reduce_all(
+        [spread_out(qkv_grad), small_grad.astype(BF16)],
+        order,
+        lines,
+        3,
+        carry=(fc_grad, proj_grad, out_grad),
     )
     small_grad = small_grad.reshape(2 * sixteen, -1)[:small_rows, :shard].astype(F32)
 

time: 270 us -> 257 us (0.952)
  Pallas kernels: 210 us -> 194 us
    pallas_call x2, Pallas kernels: 122 us -> 106 us  [reduce_all(): pl.pallas_call(partial(reduce_kernel, order, lines, count, len(carry), (l...]
where the time goes in v4:
time: 257 us; the launch traced here: 253 us
  Pallas kernels  194 us (75%)
  matrix products  31.8 us (12%)
  other arithmetic  14.2 us (6%)
  local copies, waits for them, and re-layouts  11.6 us (5%)
    pallas_call x2, Pallas kernels, reduce_all(): pl.pallas_call(partial(reduce_kernel, order, lines, count, len(carry), (l...  106 us
    pallas_call x2, Pallas kernels, gather_all(): pl.pallas_call(partial(gather_kernel, order, lines, count, (len(side), le...  87.7 us
    dot_general x4, matrix products, dot_rows(): return lax.dot_general(left, right, ROW_DOT, preferred_element_type=F32)  12.7 us
    dot_general x4, matrix products, dot(): return jnp.dot(left, right, preferred_element_type=F32)  10.6 us
    dot_general x4, matrix products, dot_lanes(): return lax.dot_general(left, right, LANE_DOT, preferred_element_type=F32)  8.5 us
    convert_element_type x4, other arithmetic, own(): return reduced[:, :part].reshape(weight.shape).astype(F32)  6.93 us

profile of v4, /device:TPU:0, one launch (start us, length us, event | category | flops | bytes accessed | tf_op | source)
XLA Modules:
  0.0 253.2 jit_solution(1156498915438801521)
XLA Ops:
  0.6 0.8 reshape.344
  1.4 0.8 concatenate.15
  2.2 1.0 copy-done.5
  3.2 30.1 %shard_map.254 = (bf16[8,2,48,2304]{3,2,1,0:T(8,128)(2,1)S(1)}, bf16[8,2,16,128]{3,2,1,0:T(8,128)(2,1)S(1)}) custom-call(bf16[2,48,2304]{2,1,0:T(8,128)(2,1)S(1)} %bitcast.128, bf16[2,16,128]{2,1,0:T(8,128)(2,1)S(1)} %bitcast.130), custom_call_target="tpu_custom_call" | custom-call | tf_op jit(solution)/shard_map/pallas_call | solution.py:292
  33.4 1.8 copy-done.9
  35.1 0.1 slice_reduce_fusion.2
  35.3 0.7 select_reduce_fusion.1
  36.1 0.1 copy.34
  36.3 0.8 select_reduce_fusion
  37.5 1.1 convert_reduce_fusion
  38.6 1.2 fusion.28
  39.9 3.4 %fusion.2 = bf16[256,2304]{1,0:T(8,128)(2,1)S(1)} fusion(bf16[768,2304]{1,0:T(8,128)(2,1)} %bitcast.132, f32[2304]{0:T(1024)S(1)} %pad_maximum_fusion.1, bf16[1,256,768]{2,1,0:T(8,128)(2,1)} %param.15, f32[768]{0:T(1024)S(1)} %add.193, f32[768]{0:T(1024)S(1)} %mul.192, f32[256]{0:T(256)S(1)} %add_rsqrt_fusion.1, f32[256]{0:T(256)S(1)} %broadcast_multiply_fusion.6), kind=kOutput, calls=%fused_computation.10 | convolution fusion | flops 908328960 | bytes 5129216 | tf_op jit(solution)/shard_map/dot_general | solution.py:21
  43.5 57.6 %shard_map.255 = (bf16[8,2,48,3072]{3,2,1,0:T(8,128)(2,1)}, bf16[8,2,192,768]{3,2,1,0:T(8,128)(2,1)}, bf16[8,2,48,768]{3,2,1,0:T(8,128)(2,1)S(1)}, bf16[4,256,15...) custom-call(bf16[2,48,3072]{2,1,0:T(8,128)(2,1)S(1)} %bitcast.126, ...), custom_call_target="tpu_custom_call" | custom-call | tf_op jit(solution)/shard_map/pallas_call | solution.py:292
  101.2 0.6 fusion.61
  101.8 0.7 add.212
  102.7 0.2 multiply_reduce_fusion.2
  102.9 4.0 %convolution_add_fusion.1 = f32[256,3072]{1,0:T(8,128)S(1)} fusion(bf16[768,3072]{1,0:T(8,128)(2,1)} %bitcast.149, f32[3072]{0:T(1024)S(1)} %add.206, f32[256,768]{1,0:T(8,128)S(1)} %get-tuple-element.77, f32[768]{0:T(1024)S(1)} %add.203, f32[768]{0:T(1024)S(1)} %mul.198, f32[256]{0:T(256)S(1)} %add_rsqrt_fusion, f32[256]{0:T(256)S(1)} %broadcast_multiply_fusion.5), kind=kOutput, calls=%fused_computation.8 | convolution fusion | flops 1209729024 | bytes 8671232 | tf_op jit(solution)/shard_map/dot_general | solution.py:21
  107.0 2.7 %fusion.12 = bf16[1,256,768]{2,1,0:T(8,128)(2,1)} fusion(f32[256,768]{1,0:T(8,128)S(1)} %get-tuple-element.77, bf16[3072,768]{1,0:T(8,128)(2,1)S(1)} %bitcast.155, f32[768]{0:T(1024)S(1)} %copy-done.20, f32[256,3072]{1,0:T(8,128)S(1)} %convolution_add_fusion.1), kind=kOutput, calls=%fused_computation.25 | convolution fusion | flops 1215627264 | bytes 9047040 | tf_op jit(solution)/shard_map/dot_general | solution.py:21
  109.7 3.8 %fusion.62 = (bf16[3072]{0:T(1024)(128)(2,1)}, bf16[256,3072]{1,0:T(8,128)(2,1)S(1)}) fusion(f32[256,3072]{1,0:T(8,128)S(1)} %convolution_add_fusion.1, bf16[3072,768]{1,0:T(8,128)(2,1)S(1)} %bitcast.156, bf16[1,256,768]{2,1,0:T(8,128)(2,1)S(1)} %copy-done.12), kind=kOutput, calls=%fused_computation.144 | convolution fusion | flops 1223685120 | bytes 9836544 | tf_op jit(solution)/shard_map/dot_general | solution.py:29
  113.5 2.2 multiply_reduce_fusion
  115.6 0.9 convert_reduce_fusion.1
  116.5 3.7 %convolution_convert_fusion.2 = bf16[768,3072]{1,0:T(8,128)(2,1)} fusion(bf16[256,3072]{1,0:T(8,128)(2,1)S(1)} %get-tuple-element.81, f32[256,768]{1,0:T(8,128)S(1)} %get-tuple-element.77, f32[768]{0:T(1024)S(1)} %add.203, f32[768]{0:T(1024)S(1)} %mul.198, f32[256]{0:T(256)S(1)} %add_rsqrt_fusion, f32[256]{0:T(256)S(1)} %broadcast_multiply_fusion.5), kind=kOutput, calls=%fused_computation.2 | convolution fusion | flops 1211301888 | bytes 7086080 | tf_op jit(solution)/shard_map/dot_general | solution.py:25
  120.2 4.4 %convolution_convert_fusion.1 = bf16[3072,768]{1,0:T(8,128)(2,1)} fusion(bf16[1,256,768]{2,1,0:T(8,128)(2,1)S(1)} %copy-done.12, f32[256,3072]{1,0:T(8,128)S(1)} %convolution_add_fusion.1), kind=kOutput, calls=%fused_computation.1 | convolution fusion | flops 1217396736 | bytes 8257536 | tf_op jit(solution)/shard_map/dot_general | solution.py:25
  124.7 1.5 convolution_convert_fusion.3
  126.2 1.3 convolution_convert_fusion.4.refs_8_
  127.5 65.2 %shard_map.256 = (bf16[48,3072]{1,0:T(8,128)(2,1)}, bf16[192,768]{1,0:T(8,128)(2,1)}, bf16[48,768]{1,0:T(8,128)(2,1)}, bf16[256,768]{1,0:T(8,128)(2,1)}, bf16[256,1536]{1,0:T(8,128)(2,1)}) custom-call(bf16[8,2,48,3072]{3,2,1,0:T(8,128)(2,1)} %bitcast.134, bf16[8,2,192,768]{3,2,1,0:T(8,128)(2,1)} %bitcast.137, bf16[8,2,48,768]{3,2,1,0:T(8,128)(2,1)} %bitcast.136, ...), custom_call_target="tpu_custom_call" | custom-call | tf_op jit(solution)/shard_map/pallas_call | solution.py:517
  192.7 1.0 constant_dynamic-update-slice_fusion.1
  193.7 1.2 constant_dynamic-update-slice_fusion
  194.9 1.3 fusion.27
  196.2 1.1 fusion.36
  197.3 3.0 %convolution_convert_fusion = bf16[768,2304]{1,0:T(8,128)(2,1)} fusion(bf16[256,2304]{1,0:T(8,128)(2,1)S(1)} %constant_dynamic-update-slice_fusion, bf16[1,256,768]{2,1,0:T(8,128)(2,1)S(1)} %copy-done.11, f32[768]{0:T(1024)S(1)} %add.193, f32[768]{0:T(1024)S(1)} %mul.192, f32[256]{0:T(256)S(1)} %copy-done.17, f32[256]{0:T(256)S(1)} %copy-done.15), kind=kOutput, calls=%fused_computation | convolution fusion | flops 908918784 | bytes 5120000 | tf_op jit(solution)/shard_map/dot_general | solution.py:25
  200.4 0.1 reshape.355
  200.5 0.1 stack.27
  200.5 0.1 stack.28
  200.6 0.2 reduce.1
  200.9 0.1 stack.29
  201.3 0.1 reduce.3
  201.4 0.1 stack.34
  201.6 0.7 pad.10.clone
  202.2 41.3 %shard_map.257 = (bf16[2,48,2304]{2,1,0:T(8,128)(2,1)}, bf16[2,16,256]{2,1,0:T(8,128)(2,1)}, bf16[2,48,3072]{2,1,0:T(8,128)(2,1)}, bf16[2,192,768]{2,1,0:T(8,128)(2,1)}, bf16[2,48,768]{2,1,0:T(8,128)(2,1)}) custom-call(bf16[48,3072]{1,0:T(8,128)(2,1)} %get-tuple-element.42.refs_0_, bf16[192,768]{1,0:T(8,128)(2,1)} %get-tuple-element.43.refs_1_, ...), custom_call_target="tpu_custom_call" | custom-call | tf_op jit(solution)/shard_map/pallas_call | solution.py:517
  243.5 0.7 slice_convert_fusion.1
  244.3 0.5 slice_bitcast_fusion.1
  244.8 2.0 bitcast_convert_fusion.2
  246.8 0.6 slice.96
  247.4 1.6 bitcast_convert_fusion.3
  249.0 2.2 bitcast_convert_fusion.1
  251.2 0.7 reshape.357
  251.8 1.1 bitcast_convert_fusion
  (100 shorter events, 1.5 us)
Async XLA Ops:
  2.2 1.0 copy-start.5
  33.4 1.8 copy-start.9
  36.3 7.1 %copy-start.2 = (s32[256,1]{1,0:T(8,128)}, s32[256,1]{1,0:T(8,128)S(1)}, u32[]{:S(2)}) copy-start(s32[256,1]{1,0:T(8,128)S(1)} %fusion.50.refs_3_) | copy-start | bytes 3076
  37.1 6.3 %copy-start.8 = (s32[1,1024]{1,0:T(1,128)}, s32[1,1024]{1,0:T(1,128)S(1)}, u32[]{:S(2)}) copy-start(s32[1,1024]{1,0:T(1,128)S(1)} %fusion.54.refs_4_) | copy-start | bytes 12292
  38.6 4.7 %copy-start.14 = (f32[256]{0:T(256)}, f32[256]{0:T(256)S(1)}, u32[]{:S(2)}) copy-start(f32[256]{0:T(256)S(1)} %broadcast_multiply_fusion.6) | copy-start | bytes 3076
  39.9 3.5 %copy-start.16 = (f32[256]{0:T(256)}, f32[256]{0:T(256)S(1)}, u32[]{:S(2)}) copy-start(f32[256]{0:T(256)S(1)} %add_rsqrt_fusion.1) | copy-start | bytes 3076
  39.9 3.6 %copy-start.3 = (bf16[96,3072]{1,0:T(8,128)(2,1)S(1)}, bf16[96,3072]{1,0:T(8,128)(2,1)}, u32[]{:S(2)}) copy-start(bf16[96,3072]{1,0:T(8,128)(2,1)} %param.26) | copy-start | bytes 1769476
  39.9 3.6 %copy-start.4 = (bf16[384,768]{1,0:T(8,128)(2,1)S(1)}, bf16[384,768]{1,0:T(8,128)(2,1)}, u32[]{:S(2)}) copy-start(bf16[384,768]{1,0:T(8,128)(2,1)} %param.28) | copy-start | bytes 1769476
  39.9 3.6 %copy-start.6 = (bf16[96,768]{1,0:T(8,128)(2,1)S(1)}, bf16[96,768]{1,0:T(8,128)(2,1)}, u32[]{:S(2)}) copy-start(bf16[96,768]{1,0:T(8,128)(2,1)} %param.22) | copy-start | bytes 442372
  43.3 57.8 %copy-start.11 = (bf16[1,256,768]{2,1,0:T(8,128)(2,1)S(1)}, bf16[1,256,768]{2,1,0:T(8,128)(2,1)}, u32[]{:S(2)}) copy-start(bf16[1,256,768]{2,1,0:T(8,128)(2,1)} %param.15) | copy-start | bytes 1179652
  43.4 58.4 %copy-start.1 = (bf16[256,768]{1,0:T(8,128)(2,1)}, bf16[256,768]{1,0:T(8,128)(2,1)S(1)}, u32[]{:S(2)}) copy-start(bf16[256,768]{1,0:T(8,128)(2,1)S(1)} %slice.88.refs_5_) | copy-start | bytes 1179652
  101.1 0.6 copy-start.7
  101.1 23.5 %copy-start = (f32[256,768]{1,0:T(8,128)}, f32[256,768]{1,0:T(8,128)S(1)}, u32[]{:S(2)}) copy-start(f32[256,768]{1,0:T(8,128)S(1)} %get-tuple-element.34.refs_7_) | copy-start | bytes 2359300
  102.7 4.2 %slice-start.2 = ((s8[4718592]{0:T(1024)(128)(4,1)}), s8[4194304]{0:T(1024)(128)(4,1)S(1)}, s32[]{:S(2)}) async-start(s8[4718592]{0:T(1024)(128)(4,1)} %bitcast.153), calls=%async_computation.2 | async-start | bytes 8388608
  102.9 4.0 %copy-start.20 = (f32[768]{0:T(1024)S(1)}, f32[768]{0:T(1024)}, u32[]{:S(2)}) copy-start(f32[768]{0:T(1024)} %add.212) | copy-start | bytes 9220
  102.9 4.0 %slice-start.3 = ((s8[4718592]{0:T(1024)(128)(4,1)}), s8[524288]{0:T(1024)(128)(4,1)S(1)}, s32[]{:S(2)}) async-start(s8[4718592]{0:T(1024)(128)(4,1)} %bitcast.153), calls=%async_computation.3 | async-start | bytes 1048576
  106.9 2.7 %copy-start.12 = (bf16[1,256,768]{2,1,0:T(8,128)(2,1)S(1)}, bf16[1,256,768]{2,1,0:T(8,128)(2,1)}, u32[]{:S(2)}) copy-start(bf16[1,256,768]{2,1,0:T(8,128)(2,1)} %param.16) | copy-start | bytes 1179652
  107.0 6.5 %slice-start = ((s8[4718592]{0:T(1024)(128)(4,1)}), s8[4194304]{0:T(1024)(128)(4,1)S(1)}, s32[]{:S(2)}) async-start(s8[4718592]{0:T(1024)(128)(4,1)} %bitcast.150), calls=%async_computation | async-start | bytes 8388608
  109.7 3.8 %slice-start.1 = ((s8[4718592]{0:T(1024)(128)(4,1)}), s8[524288]{0:T(1024)(128)(4,1)S(1)}, s32[]{:S(2)}) async-start(s8[4718592]{0:T(1024)(128)(4,1)} %bitcast.150), calls=%async_computation.1 | async-start | bytes 1048576
  127.4 67.5 %copy-start.10 = (bf16[8,2,48,2304]{3,2,1,0:T(8,128)(2,1)S(1)}, bf16[8,2,48,2304]{3,2,1,0:T(8,128)(2,1)}, u32[]{:S(2)}) copy-start(bf16[8,2,48,2304]{3,2,1,0:T(8,128)(2,1)} %copy-done.9) | copy-start | bytes 10616836
  127.4 67.5 %copy-start.15 = (f32[256]{0:T(256)S(1)}, f32[256]{0:T(256)}, u32[]{:S(2)}) copy-start(f32[256]{0:T(256)} %copy-done.14) | copy-start | bytes 3076
  127.5 67.5 %copy-start.17 = (f32[256]{0:T(256)S(1)}, f32[256]{0:T(256)}, u32[]{:S(2)}) copy-start(f32[256]{0:T(256)} %copy-done.16) | copy-start | bytes 3076
  197.3 3.1 %copy-start.19 = (bf16[3072]{0:T(1024)(128)(2,1)S(1)}, bf16[3072]{0:T(1024)(128)(2,1)}, u32[]{:S(2)}) copy-start(bf16[3072]{0:T(1024)(128)(2,1)} %get-tuple-element.80) | copy-start | bytes 18436
  197.3 3.7 %copy-start.18 = (bf16[768]{0:T(1024)(128)(2,1)S(1)}, bf16[768]{0:T(1024)(128)(2,1)}, u32[]{:S(2)}) copy-start(bf16[768]{0:T(1024)(128)(2,1)} %get-tuple-element.66) | copy-start | bytes 4612
  197.3 3.8 %copy-start.22 = (bf16[768]{0:T(1024)(128)(2,1)S(1)}, bf16[768]{0:T(1024)(128)(2,1)}, u32[]{:S(2)}) copy-start(bf16[768]{0:T(1024)(128)(2,1)} %get-tuple-element.50) | copy-start | bytes 4612
  197.3 3.9 %copy-start.21 = (bf16[768]{0:T(1024)(128)(2,1)S(1)}, bf16[768]{0:T(1024)(128)(2,1)}, u32[]{:S(2)}) copy-start(bf16[768]{0:T(1024)(128)(2,1)} %get-tuple-element.56) | copy-start | bytes 4612
  243.5 8.3 %copy-start.13 = (bf16[2,192,768]{2,1,0:T(8,128)(2,1)S(1)}, bf16[2,192,768]{2,1,0:T(8,128)(2,1)}, u32[]{:S(2)}) copy-start(bf16[2,192,768]{2,1,0:T(8,128)(2,1)} %get-tuple-element.49) | copy-start | bytes 1769476
